TPU v7x, 512 devices: a whole 4x8x8 slice. The times are simulated.
512 devices in a mesh: dp: 16 (over x_lo, y), expert: 32 (over z, x_hi, core).
Axes of the slice: x: 4 (x_hi: 2, x_lo: 2; x = x_hi * 2 + x_lo), y: 8, z: 8, core: 2. Of those that a mesh axis runs over, the one named last changes fastest.
Arguments:
- tokens: bfloat16 [65536, 1024], P(('dp', 'expert')), may hold values from -6 to 6
- cotangent: bfloat16 [65536, 1024], P(('dp', 'expert')), may hold values from -6 to 6
- gates: float32 [65536, 4], P(('dp', 'expert')), may hold values from 0.05 to 0.5
- expert_ids: int32 [65536, 4], P(('dp', 'expert')), may hold values from 0 to 31, all different within a row; in each aligned block of 128 rows (0 to 127, 128 to 255, ...) at most 24 rows name the same one
- placement: int32 [32], replicated, may hold values from 0 to 31, each once
- partner: int32 [32], replicated, may hold values from 0 to 31, as said below
- w_gate_up: bfloat16 [32, 1024, 1024], P('expert', 'dp'), may hold values from -0.1875 to 0.1875
- w_down: bfloat16 [32, 512, 1024], P('expert', 'dp'), may hold values from -0.25 to 0.25
Outputs:
- token_grad: bfloat16 [65536, 1024], P(('dp', 'expert'))
- grad_gate_up: float32 [32, 1024, 1024], P('expert', 'dp')
- grad_down: float32 [32, 512, 1024], P('expert', 'dp')
Inputs may be any that keep to these rules, and one draw needn't show every extreme that they name: `expert_ids`: within each device's aligned block of 128 rows no expert is named by more than 24 choices; the 4 entries of a row differ. `placement`: each index appears once. partner[partner[j]] = j, and partner[j] is j or differs from j in exactly one bit of its binary form.
All inputs are finite; a program needn't handle non-finite values.
Results may differ from a plain program's by a relative error of at most 0.02.
Values may be sent and summed in bfloat16 or wider, within the bound.
A program may use at most 64 MiB of HBM per device.

v0:
```python
import jax
import jax.numpy as jnp
from jax import lax
from jax.sharding import PartitionSpec as P


def partner_2(value, axis, stride):
    mask = 2**stride
    pairs = [(source, source ^ mask) for source in range(lax.axis_size(axis))]
    return lax.ppermute(value, axis, pairs)


def table_lookup(keys, table):
    hits = keys[..., None] == jnp.arange(table.shape[0], dtype=jnp.int32)
    return jnp.sum(jnp.where(hits, table, 0), axis=-1)


def rows_after(pre, grad_hidden, hidden_units):
    gate_pre = pre[:, :hidden_units]
    up_pre = pre[:, hidden_units:]
    sigma = jax.nn.sigmoid(gate_pre)
    active = gate_pre * sigma
    hidden = (active * up_pre).astype(jnp.bfloat16)
    grad_gate = grad_hidden * up_pre * (sigma * (1.0 + gate_pre * (1.0 - sigma)))
    grad_up = grad_hidden * active
    joined = jnp.concatenate([grad_gate, grad_up], axis=1).astype(jnp.bfloat16)
    return (hidden, joined)


def body(tokens, cotangent, gates, expert_ids, placement, partner, w_gate_up, w_down):
    n_exp = lax.axis_size("expert")
    here = lax.axis_index("expert")
    tok_rows, top = expert_ids.shape
    width = tokens.shape[1]
    hidden_units = w_down.shape[1] * lax.axis_size("dp")
    capacity = 3 * tok_rows * top // (2 * n_exp)
    slots = n_exp * capacity
    entries = tok_rows * top
    levels = n_exp.bit_length() - 1
    mate = lax.dynamic_slice_in_dim(partner, here, 1)[0]
    target = table_lookup(expert_ids, placement)
    flat_target = target.reshape(entries)
    onehot = (flat_target[:, None] == jnp.arange(n_exp, dtype=jnp.int32)).astype(jnp.int32)
    ahead = jnp.cumsum(onehot, axis=0) - onehot
    rank = jnp.sum(ahead * onehot, axis=1)
    slot_of = flat_target * capacity + rank
    filled = (
        jnp.zeros((slots,), jnp.int32).at[slot_of].set(jnp.arange(1, entries + 1, dtype=jnp.int32))
    )
    live = filled > 0
    source = jnp.maximum(filled - 1, 0)
    row_of = source // top
    scaled = (
        gates.reshape(entries)[source][:, None] * cotangent[row_of].astype(jnp.float32)
    ).astype(jnp.bfloat16)
    blank = jnp.zeros((), jnp.bfloat16)
    send_rows = jnp.where(live[:, None], tokens[row_of], blank).reshape(n_exp, capacity, width)
    send_up = jnp.where(live[:, None], scaled, blank).reshape(n_exp, capacity, width)
    arrived_rows, arrived_up = (
        lax.all_to_all(send_rows, "expert", split_axis=0, concat_axis=0, tiled=True),
        lax.all_to_all(send_up, "expert", split_axis=0, concat_axis=0, tiled=True),
    )
    inputs = arrived_rows.reshape(slots, width)
    upstream = arrived_up.reshape(slots, width)
    local_gu = w_gate_up
    local_dn = w_down
    for bit in range(levels):
        got_gu, got_dn = partner_2((w_gate_up, w_down), "expert", bit)
        take = mate == jnp.bitwise_xor(here, 1 << bit)
        local_gu = jnp.where(take, got_gu, local_gu)
        local_dn = jnp.where(take, got_dn, local_dn)
    contract_last = (((1,), (1,)), ((), ()))
    whole_gu, whole_dn = (
        lax.all_gather(local_gu, "dp", axis=1, tiled=True),
        lax.all_gather(local_dn, "dp", axis=1, tiled=True),
    )
    weight_gu = whole_gu[0]
    pre = jnp.dot(inputs, weight_gu, preferred_element_type=jnp.float32)
    grad_hidden = lax.dot_general(
        upstream, whole_dn[0], contract_last, preferred_element_type=jnp.float32
    )
    hidden, joined = rows_after(pre, grad_hidden, hidden_units)
    back = lax.dot_general(joined, weight_gu, contract_last, preferred_element_type=jnp.float32)
    returned = lax.all_to_all(
        back.astype(jnp.bfloat16).reshape(n_exp, capacity, width),
        "expert",
        split_axis=0,
        concat_axis=0,
        tiled=True,
    )
    picked = (
        returned.reshape(slots, width)[slot_of].astype(jnp.float32).reshape(tok_rows, top, width)
    )
    token_grad = jnp.sum(picked, axis=1).astype(jnp.bfloat16)
    contract_first = (((0,), (0,)), ((), ()))
    part_gu = lax.dot_general(inputs, joined, contract_first, preferred_element_type=jnp.float32)
    part_dn = lax.dot_general(hidden, upstream, contract_first, preferred_element_type=jnp.float32)
    share_gu, share_dn = (
        lax.psum_scatter(
            part_gu.astype(jnp.bfloat16), "dp", scatter_dimension=0, tiled=True
        ).astype(jnp.float32),
        lax.psum_scatter(
            part_dn.astype(jnp.bfloat16), "dp", scatter_dimension=0, tiled=True
        ).astype(jnp.float32),
    )
    share_gu = share_gu[None]
    share_dn = share_dn[None]
    return (token_grad, share_gu, share_dn)


def solution(mesh):
    return jax.shard_map(
        body,
        mesh=mesh,
        in_specs=(
            P(("dp", "expert"), None),
            P(("dp", "expert"), None),
            P(("dp", "expert"), None),
            P(("dp", "expert"), None),
            P(),
            P(),
            P("expert", "dp", None),
            P("expert", "dp", None),
        ),
        out_specs=(P(("dp", "expert"), None), P("expert", "dp", None), P("expert", "dp", None)),
        check_vma=False,
    )
```

profile of v0, /device:TPU:4, one launch (start us, length us, event | category | flops | bytes accessed | tf_op | source)
XLA Modules:
  0.0 398.9 jit_solution(14329271243910897861)
XLA Ops:
  7.2 0.8 select_reduce_fusion
  8.4 1.2 reduce-window.6
  9.5 0.2 slice_reduce_fusion
  10.1 2.4 scatter_custom_fusion
  12.7 0.8 copy.23
  13.6 5.0 %gather_fusion = f32[768]{0:T(1024)S(1)} fusion(f32[512]{0:T(512)S(1)} %reshape.93, s32[1024]{0:T(1024)S(1)} %get-tuple-element.10), kind=kCustom, calls=%fused_computation | custom fusion | bytes 9216 | tf_op jit(solution)/shard_map/gather | solution.py:54
  18.8 2.8 gather_fusion.2
  21.6 3.6 gather_fusion.1
  25.2 3.8 broadcast_select_fusion
  29.0 13.6 %all-to-all-start.1 = ((bf16[32,24,1024]{2,1,0:T(8,128)(2,1)}), bf16[32,24,1024]{2,1,0:T(8,128)(2,1)S(1)}, u32[]{:S(2)}, u32[]{:S(2)}) async-start(bf16[32,24,1024]{2,1,0:T(8,128)(2,1)} %get-tuple-element.5), calls=%async_computation.1 | async-start | bytes 3145728 | tf_op jit(solution)/shard_map/all_to_all | solution.py:60
  42.6 2.1 collective-permute-start.8
  44.7 3.7 collective-permute-start.7
  48.5 4.3 %collective-permute-start.6 = (bf16[1,64,1024]{2,1,0:T(8,128)(2,1)S(1)}, bf16[1,64,1024]{2,1,0:T(8,128)(2,1)S(1)}, u32[]{:S(2)}, u32[]{:S(2)}) collective-permute-start(bf16[1,64,1024]{2,1,0:T(8,128)(2,1)S(1)} %copy-done.2), channel_id=1, source_target_pairs={{0,8},{1,9},{2,10},{3,11},{4,12},{5,13},{6,14},{7,15},{8,0},{9,1},... | collective-permute-start | bytes 393224 | tf_op jit(solution)/shard_map/ppermute | solution.py:10
  52.7 4.6 %collective-permute-start.5 = (bf16[1,64,1024]{2,1,0:T(8,128)(2,1)S(1)}, bf16[1,64,1024]{2,1,0:T(8,128)(2,1)S(1)}, u32[]{:S(2)}, u32[]{:S(2)}) collective-permute-start(bf16[1,64,1024]{2,1,0:T(8,128)(2,1)S(1)} %copy-done.2), channel_id=1, source_target_pairs={{0,16},{1,17},{2,18},{3,19},{4,20},{5,21},{6,22},{7,23},{8,24},{9,... | collective-permute-start | bytes 393224 | tf_op jit(solution)/shard_map/ppermute | solution.py:10
  57.4 1.9 collective-permute-start.9
  59.3 0.6 dynamic_slice.3
  63.2 21.7 %collective-permute-done.7 = bf16[1,64,1024]{2,1,0:T(8,128)(2,1)S(1)} collective-permute-done((bf16[1,64,1024]{2,1,0:T(8,128)(2,1)S(1)}, bf16[1,64,1024]{2,1,0:T(8,128)(2,1)S(1)}, u32[]{:S(2)}, u32[]{:S(2)}) %collective-permute-start.7) | collective-permute-done | bytes 131104 | tf_op jit(solution)/shard_map/ppermute | solution.py:10
  84.9 6.5 %collective-permute-done.5 = bf16[1,64,1024]{2,1,0:T(8,128)(2,1)S(1)} collective-permute-done((bf16[1,64,1024]{2,1,0:T(8,128)(2,1)S(1)}, bf16[1,64,1024]{2,1,0:T(8,128)(2,1)S(1)}, u32[]{:S(2)}, u32[]{:S(2)}) %collective-permute-start.5) | collective-permute-done | bytes 131104 | tf_op jit(solution)/shard_map/ppermute | solution.py:10
  91.4 0.7 select_select_fusion
  92.2 7.8 %all-to-all-start = ((bf16[32,24,1024]{2,1,0:T(8,128)(2,1)}), bf16[32,24,1024]{2,1,0:T(8,128)(2,1)S(1)}, u32[]{:S(2)}, u32[]{:S(2)}) async-start(bf16[32,24,1024]{2,1,0:T(8,128)(2,1)} %get-tuple-element.6), calls=%async_computation | async-start | bytes 3145728 | tf_op jit(solution)/shard_map/all_to_all | solution.py:61
  100.0 2.1 collective-permute-start.3
  102.2 3.7 collective-permute-start.2
  105.9 4.3 %collective-permute-start.1 = (bf16[1,32,1024]{2,1,0:T(8,128)(2,1)S(1)}, bf16[1,32,1024]{2,1,0:T(8,128)(2,1)S(1)}, u32[]{:S(2)}, u32[]{:S(2)}) collective-permute-start(bf16[1,32,1024]{2,1,0:T(8,128)(2,1)S(1)} %copy-done.3), channel_id=1, source_target_pairs={{0,8},{1,9},{2,10},{3,11},{4,12},{5,13},{6,14},{7,15},{8,0},{9,1},... | collective-permute-start | bytes 196616 | tf_op jit(solution)/shard_map/ppermute | solution.py:10
  110.1 4.6 %collective-permute-start = (bf16[1,32,1024]{2,1,0:T(8,128)(2,1)S(1)}, bf16[1,32,1024]{2,1,0:T(8,128)(2,1)S(1)}, u32[]{:S(2)}, u32[]{:S(2)}) collective-permute-start(bf16[1,32,1024]{2,1,0:T(8,128)(2,1)S(1)} %copy-done.3), channel_id=1, source_target_pairs={{0,16},{1,17},{2,18},{3,19},{4,20},{5,21},{6,22},{7,23},{8,24},{9,... | collective-permute-start | bytes 196616 | tf_op jit(solution)/shard_map/ppermute | solution.py:10
  114.8 1.9 collective-permute-start.4
  116.7 1.8 collective-permute-done.3
  118.5 21.5 %collective-permute-done.2 = bf16[1,32,1024]{2,1,0:T(8,128)(2,1)S(1)} collective-permute-done((bf16[1,32,1024]{2,1,0:T(8,128)(2,1)S(1)}, bf16[1,32,1024]{2,1,0:T(8,128)(2,1)S(1)}, u32[]{:S(2)}, u32[]{:S(2)}) %collective-permute-start.2) | collective-permute-done | bytes 65568 | tf_op jit(solution)/shard_map/ppermute | solution.py:10
  140.1 4.3 %collective-permute-done = bf16[1,32,1024]{2,1,0:T(8,128)(2,1)S(1)} collective-permute-done((bf16[1,32,1024]{2,1,0:T(8,128)(2,1)S(1)}, bf16[1,32,1024]{2,1,0:T(8,128)(2,1)S(1)}, u32[]{:S(2)}, u32[]{:S(2)}) %collective-permute-start) | collective-permute-done | bytes 65568 | tf_op jit(solution)/shard_map/ppermute | solution.py:10
  144.4 0.7 select_select_fusion.1
  145.1 22.9 %all-gather.5.cloned.1.call-done = bf16[1,1024,1024]{2,1,0:T(8,128)(2,1)} async-done(((bf16[1,64,1024]{2,1,0:T(8,128)(2,1)}), bf16[1,1024,1024]{2,1,0:T(8,128)(2,1)}) %all-gather.5.cloned.1.call-update) | async-done | bytes 2097168 | tf_op jit(solution)/shard_map/all_gather | solution.py:74
  168.0 5.2 %fusion.3 = f32[768,1024]{0,1:T(8,128)} fusion(bf16[768,1024]{1,0:T(8,128)(2,1)S(1)} %bitcast.55, bf16[1,1024,1024]{2,1,0:T(8,128)(2,1)} %all-gather.5.cloned.1.call-done), kind=kOutput, calls=%fused_computation.9 | convolution fusion | flops 1610612736 | bytes 6815744 | tf_op jit(solution)/shard_map/dot_general | solution.py:78
  173.2 3.9 convolution_convert_fusion.1
  177.3 61.7 %all-gather.3.cloned.1.call-done = bf16[1,512,1024]{2,1,0:T(8,128)(2,1)} async-done(((bf16[1,32,1024]{2,1,0:T(8,128)(2,1)}), bf16[1,512,1024]{2,1,0:T(8,128)(2,1)}) %all-gather.3.cloned.1.call-update) | async-done | bytes 1048592 | tf_op jit(solution)/shard_map/all_gather | solution.py:75
  239.0 3.7 multiply_convert_fusion.2
  242.7 0.9 copy-done.5
  243.6 0.3 copy-done.7
  243.8 3.2 convolution_convert_fusion
  247.1 1.1 copy-done.6
  248.2 0.2 copy-done.8
  248.4 4.6 %fusion.5 = bf16[768,1024]{1,0:T(8,128)(2,1)} fusion(bf16[1,1024,1024]{2,1,0:T(8,128)(2,1)} %all-gather.5.cloned.1.call-done, bf16[768,512]{0,1:T(8,128)(2,1)S(1)} %copy-done.8, bf16[768,512]{0,1:T(8,128)(2,1)S(1)} %copy-done.6), kind=kOutput, calls=%fused_computation.12 | convolution fusion | flops 1614544896 | bytes 5242880 | tf_op jit(solution)/shard_map/dot_general | solution.py:83
  253.0 10.4 %all-to-all-start.2 = ((bf16[32,24,1024]{2,1,0:T(8,128)(2,1)}), bf16[32,24,1024]{2,1,0:T(8,128)(2,1)S(1)}, u32[]{:S(2)}, u32[]{:S(2)}) async-start(bf16[32,24,1024]{2,1,0:T(8,128)(2,1)} %bitcast.10), calls=%async_computation.2 | async-start | bytes 3145728 | tf_op jit(solution)/shard_map/all_to_all | solution.py:84
  263.4 51.4 %reduce-scatter.5.cloned.1.call-done = bf16[32,1024]{1,0:T(8,128)(2,1)} async-done(((bf16[512,1024]{1,0:T(8,128)(2,1)}), bf16[32,1024]{1,0:T(8,128)(2,1)}) %reduce-scatter.5.cloned.1.call-update) | async-done | bytes 65552 | tf_op jit(solution)/shard_map/reduce_scatter | solution.py:102
  314.8 1.5 bitcast_convert_fusion.1
  316.3 2.1 gather_fusion.3
  318.4 0.4 gather.21
  318.8 2.1 reduce_sum.35
  320.9 69.8 %reduce-scatter.3.cloned.1.call-done = bf16[64,1024]{1,0:T(8,128)(2,1)} async-done(((bf16[1024,1024]{1,0:T(8,128)(2,1)}), bf16[64,1024]{1,0:T(8,128)(2,1)}) %reduce-scatter.3.cloned.1.call-update) | async-done | bytes 131088 | tf_op jit(solution)/shard_map/reduce_scatter | solution.py:99
  390.7 1.6 bitcast_convert_fusion
  (49 shorter events, 1.5 us)
Async XLA Ops:
  7.2 11.6 %copy-start = (bf16[128,1024]{1,0:T(8,128)(2,1)S(1)}, bf16[128,1024]{1,0:T(8,128)(2,1)}, u32[]{:S(2)}) copy-start(bf16[128,1024]{1,0:T(8,128)(2,1)} %param.8) | copy-start | bytes 786436
  18.7 2.8 copy-start.1
  29.0 13.6 %copy-start.2 = (bf16[1,64,1024]{2,1,0:T(8,128)(2,1)S(1)}, bf16[1,64,1024]{2,1,0:T(8,128)(2,1)}, u32[]{:S(2)}) copy-start(bf16[1,64,1024]{2,1,0:T(8,128)(2,1)} %param.14) | copy-start | bytes 393220
  29.0 30.4 %copy-start.4 = (s32[32]{0:T(128)S(1)}, s32[32]{0:T(128)}, u32[]{:S(2)}) copy-start(s32[32]{0:T(128)} %param.13) | copy-start | bytes 388
  29.0 63.2 %all-to-all-start.1 = ((bf16[32,24,1024]{2,1,0:T(8,128)(2,1)}), bf16[32,24,1024]{2,1,0:T(8,128)(2,1)S(1)}, u32[]{:S(2)}, u32[]{:S(2)}) async-start(bf16[32,24,1024]{2,1,0:T(8,128)(2,1)} %get-tuple-element.5), calls=%async_computation.1 | async-start | bytes 3145728 | tf_op jit(solution)/shard_map/all_to_all | solution.py:60
  42.5 125.5 %all-gather.5.cloned.1.call-start = ((), (), s32[]{:S(2)}) async-start(), calls=%async_computation.6 | async-start | bytes 2228224 | tf_op jit(solution)/shard_map/all_gather | solution.py:74
  42.6 20.6 %collective-permute-start.8 = (bf16[1,64,1024]{2,1,0:T(8,128)(2,1)S(1)}, bf16[1,64,1024]{2,1,0:T(8,128)(2,1)S(1)}, u32[]{:S(2)}, u32[]{:S(2)}) collective-permute-start(bf16[1,64,1024]{2,1,0:T(8,128)(2,1)S(1)} %copy-done.2), channel_id=1, source_target_pairs={{0,2},{1,3},{2,0},{3,1},{4,6},{5,7},{6,4},{7,5},{8,10},{9,11},{10,... | collective-permute-start | bytes 393224 | tf_op jit(solution)/shard_map/ppermute | solution.py:10
  44.7 40.1 %collective-permute-start.7 = (bf16[1,64,1024]{2,1,0:T(8,128)(2,1)S(1)}, bf16[1,64,1024]{2,1,0:T(8,128)(2,1)S(1)}, u32[]{:S(2)}, u32[]{:S(2)}) collective-permute-start(bf16[1,64,1024]{2,1,0:T(8,128)(2,1)S(1)} %copy-done.2), channel_id=1, source_target_pairs={{0,4},{1,5},{2,6},{3,7},{4,0},{5,1},{6,2},{7,3},{8,12},{9,13},{10,... | collective-permute-start | bytes 393224 | tf_op jit(solution)/shard_map/ppermute | solution.py:10
  48.5 36.4 %collective-permute-start.6 = (bf16[1,64,1024]{2,1,0:T(8,128)(2,1)S(1)}, bf16[1,64,1024]{2,1,0:T(8,128)(2,1)S(1)}, u32[]{:S(2)}, u32[]{:S(2)}) collective-permute-start(bf16[1,64,1024]{2,1,0:T(8,128)(2,1)S(1)} %copy-done.2), channel_id=1, source_target_pairs={{0,8},{1,9},{2,10},{3,11},{4,12},{5,13},{6,14},{7,15},{8,0},{9,1},... | collective-permute-start | bytes 393224 | tf_op jit(solution)/shard_map/ppermute | solution.py:10
  52.7 38.7 %collective-permute-start.5 = (bf16[1,64,1024]{2,1,0:T(8,128)(2,1)S(1)}, bf16[1,64,1024]{2,1,0:T(8,128)(2,1)S(1)}, u32[]{:S(2)}, u32[]{:S(2)}) collective-permute-start(bf16[1,64,1024]{2,1,0:T(8,128)(2,1)S(1)} %copy-done.2), channel_id=1, source_target_pairs={{0,16},{1,17},{2,18},{3,19},{4,20},{5,21},{6,22},{7,23},{8,24},{9,... | collective-permute-start | bytes 393224 | tf_op jit(solution)/shard_map/ppermute | solution.py:10
  57.4 34.0 %collective-permute-start.9 = (bf16[1,64,1024]{2,1,0:T(8,128)(2,1)S(1)}, bf16[1,64,1024]{2,1,0:T(8,128)(2,1)S(1)}, u32[]{:S(2)}, u32[]{:S(2)}) collective-permute-start(bf16[1,64,1024]{2,1,0:T(8,128)(2,1)S(1)} %copy-done.2), channel_id=1, source_target_pairs={{0,1},{1,0},{2,3},{3,2},{4,5},{5,4},{6,7},{7,6},{8,9},{9,8},{10,11... | collective-permute-start | bytes 393224 | tf_op jit(solution)/shard_map/ppermute | solution.py:10
  92.2 7.8 %copy-start.3 = (bf16[1,32,1024]{2,1,0:T(8,128)(2,1)S(1)}, bf16[1,32,1024]{2,1,0:T(8,128)(2,1)}, u32[]{:S(2)}) copy-start(bf16[1,32,1024]{2,1,0:T(8,128)(2,1)} %param.15) | copy-start | bytes 196612
  92.2 81.0 %all-to-all-start = ((bf16[32,24,1024]{2,1,0:T(8,128)(2,1)}), bf16[32,24,1024]{2,1,0:T(8,128)(2,1)S(1)}, u32[]{:S(2)}, u32[]{:S(2)}) async-start(bf16[32,24,1024]{2,1,0:T(8,128)(2,1)} %get-tuple-element.6), calls=%async_computation | async-start | bytes 3145728 | tf_op jit(solution)/shard_map/all_to_all | solution.py:61
  99.9 139.1 %all-gather.3.cloned.1.call-start = ((), (), s32[]{:S(2)}) async-start(), calls=%async_computation.5 | async-start | bytes 1114112 | tf_op jit(solution)/shard_map/all_gather | solution.py:75
  100.0 18.5 %collective-permute-start.3 = (bf16[1,32,1024]{2,1,0:T(8,128)(2,1)S(1)}, bf16[1,32,1024]{2,1,0:T(8,128)(2,1)S(1)}, u32[]{:S(2)}, u32[]{:S(2)}) collective-permute-start(bf16[1,32,1024]{2,1,0:T(8,128)(2,1)S(1)} %copy-done.3), channel_id=1, source_target_pairs={{0,2},{1,3},{2,0},{3,1},{4,6},{5,7},{6,4},{7,5},{8,10},{9,11},{10,... | collective-permute-start | bytes 196616 | tf_op jit(solution)/shard_map/ppermute | solution.py:10
  102.2 37.9 %collective-permute-start.2 = (bf16[1,32,1024]{2,1,0:T(8,128)(2,1)S(1)}, bf16[1,32,1024]{2,1,0:T(8,128)(2,1)S(1)}, u32[]{:S(2)}, u32[]{:S(2)}) collective-permute-start(bf16[1,32,1024]{2,1,0:T(8,128)(2,1)S(1)} %copy-done.3), channel_id=1, source_target_pairs={{0,4},{1,5},{2,6},{3,7},{4,0},{5,1},{6,2},{7,3},{8,12},{9,13},{10,... | collective-permute-start | bytes 196616 | tf_op jit(solution)/shard_map/ppermute | solution.py:10
  105.9 34.2 %collective-permute-start.1 = (bf16[1,32,1024]{2,1,0:T(8,128)(2,1)S(1)}, bf16[1,32,1024]{2,1,0:T(8,128)(2,1)S(1)}, u32[]{:S(2)}, u32[]{:S(2)}) collective-permute-start(bf16[1,32,1024]{2,1,0:T(8,128)(2,1)S(1)} %copy-done.3), channel_id=1, source_target_pairs={{0,8},{1,9},{2,10},{3,11},{4,12},{5,13},{6,14},{7,15},{8,0},{9,1},... | collective-permute-start | bytes 196616 | tf_op jit(solution)/shard_map/ppermute | solution.py:10
  110.1 34.3 %collective-permute-start = (bf16[1,32,1024]{2,1,0:T(8,128)(2,1)S(1)}, bf16[1,32,1024]{2,1,0:T(8,128)(2,1)S(1)}, u32[]{:S(2)}, u32[]{:S(2)}) collective-permute-start(bf16[1,32,1024]{2,1,0:T(8,128)(2,1)S(1)} %copy-done.3), channel_id=1, source_target_pairs={{0,16},{1,17},{2,18},{3,19},{4,20},{5,21},{6,22},{7,23},{8,24},{9,... | collective-permute-start | bytes 196616 | tf_op jit(solution)/shard_map/ppermute | solution.py:10
  114.8 29.6 %collective-permute-start.4 = (bf16[1,32,1024]{2,1,0:T(8,128)(2,1)S(1)}, bf16[1,32,1024]{2,1,0:T(8,128)(2,1)S(1)}, u32[]{:S(2)}, u32[]{:S(2)}) collective-permute-start(bf16[1,32,1024]{2,1,0:T(8,128)(2,1)S(1)} %copy-done.3), channel_id=1, source_target_pairs={{0,1},{1,0},{2,3},{3,2},{4,5},{5,4},{6,7},{7,6},{8,9},{9,8},{10,11... | collective-permute-start | bytes 196616 | tf_op jit(solution)/shard_map/ppermute | solution.py:10
  145.1 169.7 %reduce-scatter.5.cloned.1.call-start = ((), (), s32[]{:S(2)}) async-start(), calls=%async_computation.8 | async-start | bytes 1114112 | tf_op jit(solution)/shard_map/reduce_scatter | solution.py:102
  177.1 213.7 %reduce-scatter.3.cloned.1.call-start = ((), (), s32[]{:S(2)}) async-start(), calls=%async_computation.7 | async-start | bytes 2228224 | tf_op jit(solution)/shard_map/reduce_scatter | solution.py:99
  242.7 0.9 copy-start.5
  242.7 1.2 copy-start.7
  247.1 1.1 copy-start.6
  247.1 1.4 copy-start.8
  253.0 63.3 %all-to-all-start.2 = ((bf16[32,24,1024]{2,1,0:T(8,128)(2,1)}), bf16[32,24,1024]{2,1,0:T(8,128)(2,1)S(1)}, u32[]{:S(2)}, u32[]{:S(2)}) async-start(bf16[32,24,1024]{2,1,0:T(8,128)(2,1)} %bitcast.10), calls=%async_computation.2 | async-start | bytes 3145728 | tf_op jit(solution)/shard_map/all_to_all | solution.py:84
Sparse Core Ops, SparseCore 0:
  92.3 75.6 all-gather.4
  170.7 68.3 all-gather.2
  241.8 72.9 reduce-scatter.4
  317.7 72.9 reduce-scatter.2
where the time goes:
time: 400 us; the launch traced here: 399 us
  waiting for transfers between devices  262 us (66%)
  starting transfers between devices  65.4 us (16%)
  local copies, waits for them, and re-layouts  21.3 us (5%)
  matrix products  20.6 us (5%)
  between operations  17.3 us (4%)
  other arithmetic  12.6 us (3%)
    reduce_scatter x1, waiting for transfers between devices, body(): lax.psum_scatter(part_gu.astype(jnp.bfloat16), 'dp', scatter_dimension=0,...  69.8 us
    all_gather x1, waiting for transfers between devices, body(): lax.all_gather(local_dn, 'dp', axis=1, tiled=True)  61.7 us
    ppermute x10, waiting for transfers between devices, partner_2(): return lax.ppermute(value, axis, pairs)  55.9 us
    reduce_scatter x1, waiting for transfers between devices, body(): lax.psum_scatter(part_dn.astype(jnp.bfloat16), 'dp', scatter_dimension=0,...  51.4 us
    ppermute x10, starting transfers between devices, partner_2(): return lax.ppermute(value, axis, pairs)  33.4 us
    all_gather x1, waiting for transfers between devices, body(): lax.all_gather(local_gu, 'dp', axis=1, tiled=True)  22.9 us
    all_to_all x1, starting transfers between devices, body(): lax.all_to_all(send_rows, 'expert', split_axis=0, concat_axis=0, tiled=True)  13.6 us
    all_to_all x1, starting transfers between devices, body(): lax.all_to_all(back.astype(jnp.bfloat16).reshape(n_exp, capacity, width),...  10.4 us
  transfers between devices with their start and end apart: 17, of which 9 were waited for; matrix products, arithmetic and copies ran while one was open for 7% of the time, Pallas kernels for 0%

commit v1 on v0

v1 whole, which is shorter than its diff:
```python
import functools

import jax
import jax.numpy as jnp
from jax import lax
from jax.experimental import pallas as pl
from jax.experimental.pallas import tpu as pltpu
from jax.sharding import PartitionSpec as P

MESH = pl.DeviceIdType.MESH
BF16 = jnp.bfloat16
F32 = jnp.float32

NZ = 8
NY = 8
CAP = 24
PAIR = 2 * CAP
ROWS = 4 * PAIR
TOK = 128
WIDTH = 1024
FF = 512
GU = 64
DN = 32
SEMS = 160

BEHIND = {1: 0, 2: 2, 3: 4, 4: 6, 5: 5, 6: 3, 7: 1}
AHEAD = {1: 1, 2: 3, 3: 5, 4: 6, 5: 4, 6: 2, 7: 0}
OPPOSITE, OWN = 6, 7


def flip(value, bit):
    size = 1 << bit
    return value + size - 2 * size * (lax.rem(lax.div(value, size), 2))


def dot(a, b, dims):
    return lax.dot_general(a, b, (dims, ((), ())), preferred_element_type=F32)


ROWS_COLS = ((1,), (0,))
LAST_LAST = ((1,), (1,))
FIRST_FIRST = ((0,), (0,))


def kernel(
    meta_ref, tok_ref, cot_ref, gu_ref, dn_ref, mate_ref,
    tg_out, gu_out, dn_out,
    gx, gc, gm, tri, sel, gcol, stx, stu, ex, eu, wgu, wdn, hb, qb, bk, rb,
    tgp, sz, rz, pgu, pdn, rygu, rydn, txgu, txdn, rxgu, rxdn, slgu, sldn, rlgu, rldn,
    ssem, rsem,
):
    dpi = lax.axis_index("dp")
    ei = lax.axis_index("expert")
    xl, y = lax.div(dpi, NY), lax.rem(dpi, NY)
    z, c = lax.div(ei, 4), lax.rem(ei, 4)

    def ydev(delta):
        return (xl * NY + lax.rem(y + delta + NY, NY), ei)

    def zdev(delta):
        return (dpi, lax.rem(z + delta + NZ, NZ) * 4 + c)

    column = [c, flip(c, 0), flip(c, 1), flip(flip(c, 0), 1)]
    plane = [(dpi, z * 4 + q) for q in column]
    other_side = ((1 - xl) * NY + y, ei)
    mates = [(dpi, flip(ei, bit)) for bit in range(5)]

    barrier = pltpu.get_barrier_semaphore()
    peers = [zdev(1), zdev(-1), mates[3], mates[4]] + plane[1:] + [ydev(1), ydev(-1), other_side]
    for peer in peers:
        pl.semaphore_signal(barrier, inc=1, device_id=peer, device_id_type=MESH)
    pl.semaphore_wait(barrier, len(peers))

    sent = []

    def send(src, dst, device, arrives=None):
        number = len(sent)
        copy = pltpu.make_async_remote_copy(
            src_ref=src,
            dst_ref=dst,
            send_sem=ssem.at[number],
            recv_sem=rsem.at[number],
            device_id=device,
            device_id_type=MESH,
        )
        copy.start()
        sent.append(copy)
        if arrives is None:
            return copy
        return pltpu.make_async_remote_copy(
            src_ref=arrives,
            dst_ref=arrives,
            send_sem=ssem.at[number],
            recv_sem=rsem.at[number],
            device_id=device,
            device_id_type=MESH,
        )

    def slice_at(ref, rows, side, delta):
        owner = side * NY + lax.rem(y + delta + NY, NY)
        return ref.at[pl.ds(pl.multiple_of(owner * rows, rows), rows)]

    sides = {"own": xl, "oth": 1 - xl}
    whole = {"gu": (wgu, GU, gu_ref), "dn": (wdn, DN, dn_ref)}
    reach = {("own", 1): 4, ("own", -1): 3, ("oth", 1): 3, ("oth", -1): 4}
    coming = {}

    def pass_weights(side, hop):
        for way in (1, -1):
            if hop > reach[side, way]:
                continue
            for kind, (buffer, rows, mine) in whole.items():
                if hop > 1:
                    coming[side, way, hop - 1, kind].wait_recv()
                source = slice_at(buffer, rows, sides[side], -way * (hop - 1))
                first = mine if hop == 1 and side == "own" else source
                coming[side, way, hop, kind] = send(
                    first, source, ydev(way), slice_at(buffer, rows, sides[side], -way * hop)
                )

    def last_weights(side):
        for way in (1, -1):
            for kind in whole:
                coming[side, way, reach[side, way], kind].wait_recv()

    across = {}
    for kind, (buffer, rows, mine) in whole.items():
        across[kind] = send(
            mine, slice_at(buffer, rows, xl, 0), other_side, slice_at(buffer, rows, 1 - xl, 0)
        )
    pass_weights("own", 1)

    def block(ref, index):
        return ref.at[pl.ds(index * TOK, TOK)]

    ring = {}

    def pass_meta(hop):
        if hop > 1:
            ring["m", 1, hop - 1].wait_recv()
            ring["m", -1, hop - 1].wait_recv()
        for way, order in ((1, BEHIND), (-1, AHEAD)):
            if hop > 3 and way < 0:
                continue
            source = meta_ref if hop == 1 else gm.at[order[hop - 1]]
            ring["m", way, hop] = send(source, gm.at[order[hop]], zdev(way))

    def pass_block(name, hop):
        mine, buffer = {"x": (tok_ref, gx), "c": (cot_ref, gc)}[name]
        if hop > 1:
            ring[name, 1, hop - 1].wait_recv()
            ring[name, -1, hop - 1].wait_recv()
        half = TOK // 2
        for way, order in ((1, BEHIND), (-1, AHEAD)):
            source = mine if hop == 1 else block(buffer, order[hop - 1])
            target = block(buffer, order[hop])
            if hop == 4:
                part = pl.ds(0 if way > 0 else half, half)
                source, target = source.at[part], target.at[part]
            ring[name, way, hop] = send(source, target, zdev(way))

    pass_meta(1)
    pass_block("x", 1)
    pass_block("c", 1)

    gx[OWN * TOK :, :] = tok_ref[...]
    gc[OWN * TOK :, :] = cot_ref[...]
    gm[OWN] = meta_ref[...]
    for kind, (buffer, rows, mine) in whole.items():
        slice_at(buffer, rows, xl, 0)[...] = mine[...]
    before = lax.broadcasted_iota(jnp.int32, (2 * TOK, 2 * TOK), 0)
    after = lax.broadcasted_iota(jnp.int32, (2 * TOK, 2 * TOK), 1)
    same_block = lax.div(before, TOK) == lax.div(after, TOK)
    tri[...] = jnp.where(same_block & (before < after), 1.0, 0.0).astype(BF16)

    def choose(pair):
        both = jnp.concatenate([gm[2 * pair], gm[2 * pair + 1]], axis=1)
        named, weight = both[0:4], both[4:8]
        hits, scales = [], []
        for q in column:
            hit = jnp.where(named == (z * 4 + q).astype(F32), 1.0, 0.0)
            hits.append(jnp.sum(hit, axis=0, keepdims=True))
            scales.append(jnp.sum(hit * weight, axis=0, keepdims=True))
        marks = jnp.concatenate(hits + [jnp.zeros((12, 2 * TOK), F32)], axis=0)
        ranks = dot(marks.astype(BF16), tri[...], ROWS_COLS)
        slot = lax.broadcasted_iota(jnp.int32, (CAP, 2 * TOK), 0).astype(F32)
        lane = lax.broadcasted_iota(jnp.int32, (CAP, 2 * TOK), 1)
        parts, columns = [], []
        for k in range(4):
            found = (ranks[k : k + 1] == slot) & (hits[k] > 0.5)
            for half in range(2):
                here = lane < TOK if half == 0 else lane >= TOK
                part = jnp.where(found & here, 1.0, 0.0)
                parts.append(part)
                columns.append(jnp.sum(part * scales[k], axis=1, keepdims=True))
        sel[pair] = jnp.concatenate(parts, axis=0).astype(BF16)
        gcol[pair] = jnp.broadcast_to(jnp.concatenate(columns, axis=0), (ROWS, 128))

    there = {}

    def dispatch(name, pair):
        buffer, staged, arrived = {"x": (gx, stx, ex), "c": (gc, stu, eu)}[name]
        for tile in range(0, WIDTH, 512):
            cols = pl.ds(tile, 512)
            rows = dot(sel[pair], buffer[2 * pair * TOK : 2 * (pair + 1) * TOK, cols], ROWS_COLS)
            if name == "c":
                rows = gcol[pair][:, 0:1] * rows
            rows = rows.astype(BF16)
            arrived[pair * ROWS : pair * ROWS + PAIR, cols] = rows[:PAIR]
            staged[pair * 3 * PAIR : (pair + 1) * 3 * PAIR, cols] = rows[PAIR:]
        for k in (2, 3, 1):
            there[name, pair, k] = send(
                staged.at[pl.ds((pair * 3 + k - 1) * PAIR, PAIR)],
                arrived.at[pl.ds((pair * 4 + k) * PAIR, PAIR)],
                plane[k],
            )

    returned = {}

    def expert(pair):
        for name in ("x", "c"):
            for k in (1, 2, 3):
                there[name, pair, k].wait_recv()
        rows = slice(pair * ROWS, (pair + 1) * ROWS)
        for tile in range(0, FF, 256):
            cols = pl.ds(tile, 256)
            up_cols = pl.ds(FF + tile, 256)
            a = dot(ex[rows], wgu[:, cols], ROWS_COLS)
            b = dot(ex[rows], wgu[:, up_cols], ROWS_COLS)
            dh = dot(eu[rows], wdn[cols], LAST_LAST)
            s = jax.nn.sigmoid(a)
            active = a * s
            hb[rows, cols] = (active * b).astype(BF16)
            qb[rows, cols] = (dh * b * (s * (1.0 + a * (1.0 - s)))).astype(BF16)
            qb[rows, up_cols] = (dh * active).astype(BF16)
        for tile in range(0, WIDTH, 256):
            cols = pl.ds(tile, 256)
            value = dot(qb[rows], wgu[cols], LAST_LAST).astype(BF16)
            bk[rows, cols] = value
            rb[pair * ROWS : pair * ROWS + PAIR, cols] = value[:PAIR]
        for k in (2, 3, 1):
            part = pl.ds((pair * 4 + k) * PAIR, PAIR)
            returned[pair, k] = send(bk.at[part], rb.at[part], plane[k])

    def combine(pair):
        for k in (1, 2, 3):
            returned[pair, k].wait_recv()
        for tile in range(0, WIDTH, 512):
            cols = pl.ds(tile, 512)
            tgp[pair * 256 : (pair + 1) * 256, cols] = dot(
                sel[pair], rb[pair * ROWS : (pair + 1) * ROWS, cols], FIRST_FIRST
            )

    ways = ((0, 1, BEHIND), (1, -1, AHEAD))
    sums = {}

    def token_step(step):
        for index, way, order in ways:
            if step > 1:
                sums[index, step - 1].wait_recv()
            first = order[step] * TOK
            term = tgp[first : first + TOK, index * 512 : (index + 1) * 512]
            if step == 1:
                sz[index] = term.astype(BF16)
                source = sz.at[index]
            else:
                source = rz.at[index, step - 2]
                source[...] = (source[...].astype(F32) + term).astype(BF16)
            sums[index, step] = send(source, rz.at[index, step - 1], zdev(way))

    def token_last():
        for index, _, _ in ways:
            sums[index, 7].wait_recv()
            cols = slice(index * 512, (index + 1) * 512)
            total = tgp[OWN * TOK :, cols] + rz[index, 6].astype(F32)
            tg_out[:, cols] = total.astype(BF16)

    partial = {"gu": (pgu, GU, rygu), "dn": (pdn, DN, rydn)}
    lanes = {("own", 1): 0, ("own", -1): 4, ("oth", 1): 7, ("oth", -1): 10}
    chain = {}

    def grad_step(kind, side, left):
        buffer, rows, received = partial[kind]
        for way in (1, -1):
            if left > reach[side, way]:
                continue
            term = slice_at(buffer, rows, sides[side], way * left)
            if left == reach[side, way]:
                source = term
            else:
                chain[kind, side, way, left + 1].wait_recv()
                source = received.at[lanes[side, way] + left]
                source[...] = (source[...].astype(F32) + term[...].astype(F32)).astype(BF16)
            chain[kind, side, way, left] = send(
                source, received.at[lanes[side, way] + left - 1], ydev(way)
            )

    def grad_sum(kind, side):
        buffer, rows, received = partial[kind]
        total = slice_at(buffer, rows, sides[side], 0)[...].astype(F32)
        for way in (1, -1):
            chain[kind, side, way, 1].wait_recv()
            total = total + received[lanes[side, way]].astype(F32)
        return total

    crossing = {"gu": (txgu, rxgu), "dn": (txdn, rxdn)}
    swaps = {"gu": (slgu, rlgu, gu_out), "dn": (sldn, rldn, dn_out)}
    crossed, moved = {}, {}

    def grad_cross(kind):
        outgoing, incoming = crossing[kind]
        outgoing[...] = grad_sum(kind, "oth").astype(BF16)
        crossed[kind] = send(outgoing, incoming, other_side)

    def grad_swap(kind):
        staged, landed, out = swaps[kind]
        total = grad_sum(kind, "own")
        crossed[kind].wait_recv()
        total = total + crossing[kind][1][...].astype(F32)
        out[...] = total
        staged[...] = total.astype(BF16)
        for bit in (4, 3, 2, 1, 0):
            moved[kind, bit] = send(staged, landed.at[bit], mates[bit])

    def grad_last(kind):
        _, landed, out = swaps[kind]
        mate = mate_ref[0]
        value = out[...]
        for bit in range(5):
            moved[kind, bit].wait_recv()
            value = jnp.where(mate == flip(ei, bit), landed[bit].astype(F32), value)
        out[...] = value

    def arrive_side():
        for kind in whole:
            across[kind].wait_recv()

    arrive_side()
    pass_weights("oth", 1)
    pass_weights("own", 2)
    pass_meta(2)
    pass_block("x", 2)
    choose(0)
    dispatch("x", 0)
    pass_weights("oth", 2)
    pass_block("c", 2)
    dispatch("c", 0)
    pass_weights("own", 3)
    pass_meta(3)
    pass_block("x", 3)
    choose(1)
    dispatch("x", 1)
    pass_weights("oth", 3)
    pass_block("c", 3)
    dispatch("c", 1)
    pass_weights("own", 4)
    pass_weights("oth", 4)
    pass_meta(4)
    pass_block("x", 4)
    choose(2)
    dispatch("x", 2)
    last_weights("own")
    last_weights("oth")
    ring["m", 1, 4].wait_recv()
    choose(3)
    pass_block("c", 4)
    dispatch("c", 2)
    expert(0)
    for way in (1, -1):
        ring["x", way, 4].wait_recv()
    dispatch("x", 3)
    for way in (1, -1):
        ring["c", way, 4].wait_recv()
    dispatch("c", 3)
    expert(1)
    expert(2)
    combine(0)
    token_step(1)
    combine(1)
    token_step(2)
    expert(3)
    for tile in range(0, FF, 256):
        cols = pl.ds(tile, 256)
        pdn[cols, :] = dot(hb[:, cols], eu[...], FIRST_FIRST).astype(BF16)
    grad_step("dn", "oth", 4)
    grad_step("dn", "own", 4)
    grad_step("dn", "oth", 3)
    grad_step("dn", "own", 3)
    for tile in range(0, WIDTH, 256):
        cols = pl.ds(tile, 256)
        pgu[cols, :] = dot(ex[:, cols], qb[...], FIRST_FIRST).astype(BF16)
    grad_step("gu", "oth", 4)
    grad_step("gu", "own", 4)
    grad_step("gu", "oth", 3)
    grad_step("gu", "own", 3)
    combine(2)
    token_step(3)
    combine(3)
    token_step(4)
    grad_step("dn", "oth", 2)
    grad_step("dn", "own", 2)
    token_step(5)
    grad_step("gu", "oth", 2)
    grad_step("gu", "own", 2)
    token_step(6)
    grad_step("dn", "oth", 1)
    grad_step("dn", "own", 1)
    token_step(7)
    grad_step("gu", "oth", 1)
    grad_step("gu", "own", 1)
    token_last()
    grad_cross("dn")
    grad_swap("dn")
    grad_cross("gu")
    grad_swap("gu")
    grad_last("dn")
    grad_last("gu")
    for copy in sent:
        copy.wait_send()
    assert len(sent) <= SEMS


def table_lookup(keys, table):
    hits = keys[..., None] == jnp.arange(table.shape[0], dtype=jnp.int32)
    return jnp.sum(jnp.where(hits, table, 0), axis=-1)


def body(tokens, cotangent, gates, expert_ids, placement, partner, w_gate_up, w_down):
    here = lax.axis_index("expert")
    mate = lax.dynamic_slice_in_dim(partner, here, 1)
    holder = table_lookup(expert_ids, table_lookup(placement, partner))
    meta = jnp.concatenate([holder.astype(F32).T, gates.T], axis=0)

    def vmem(*shape, dtype=BF16):
        return pltpu.VMEM(shape, dtype)

    slots = 4 * ROWS
    scratch = [
        vmem(NZ * TOK, WIDTH),
        vmem(NZ * TOK, WIDTH),
        vmem(NZ, 8, TOK, dtype=F32),
        vmem(2 * TOK, 2 * TOK),
        vmem(4, ROWS, 2 * TOK),
        vmem(4, ROWS, 128, dtype=F32),
        vmem(12 * PAIR, WIDTH),
        vmem(12 * PAIR, WIDTH),
        vmem(slots, WIDTH),
        vmem(slots, WIDTH),
        vmem(WIDTH, 2 * FF),
        vmem(FF, WIDTH),
        vmem(slots, FF),
        vmem(slots, 2 * FF),
        vmem(slots, WIDTH),
        vmem(slots, WIDTH),
        vmem(NZ * TOK, WIDTH, dtype=F32),
        vmem(2, TOK, 512),
        vmem(2, 7, TOK, 512),
        vmem(WIDTH, 2 * FF),
        vmem(FF, WIDTH),
        vmem(14, GU, 2 * FF),
        vmem(14, DN, WIDTH),
        vmem(GU, 2 * FF),
        vmem(DN, WIDTH),
        vmem(GU, 2 * FF),
        vmem(DN, WIDTH),
        vmem(GU, 2 * FF),
        vmem(DN, WIDTH),
        vmem(5, GU, 2 * FF),
        vmem(5, DN, WIDTH),
        pltpu.SemaphoreType.DMA((SEMS,)),
        pltpu.SemaphoreType.DMA((SEMS,)),
    ]
    in_vmem = pl.BlockSpec(memory_space=pltpu.VMEM)
    token_grad, grad_gu, grad_dn = pl.pallas_call(
        kernel,
        out_shape=(
            jax.ShapeDtypeStruct((TOK, WIDTH), BF16),
            jax.ShapeDtypeStruct((GU, 2 * FF), F32),
            jax.ShapeDtypeStruct((DN, WIDTH), F32),
        ),
        in_specs=[in_vmem] * 5 + [pl.BlockSpec(memory_space=pltpu.SMEM)],
        out_specs=(in_vmem,) * 3,
        scratch_shapes=scratch,
        compiler_params=pltpu.CompilerParams(
            collective_id=0, has_side_effects=True, vmem_limit_bytes=56 * 1024 * 1024
        ),
    )(meta, tokens, cotangent, w_gate_up[0], w_down[0], mate)
    return token_grad, grad_gu[None], grad_dn[None]


def solution(mesh):
    return jax.shard_map(
        body,
        mesh=mesh,
        in_specs=(
            P(("dp", "expert"), None),
            P(("dp", "expert"), None),
            P(("dp", "expert"), None),
            P(("dp", "expert"), None),
            P(),
            P(),
            P("expert", "dp", None),
            P("expert", "dp", None),
        ),
        out_specs=(P(("dp", "expert"), None), P("expert", "dp", None), P("expert", "dp", None)),
        check_vma=False,
    )
```

time: 400 us -> 145 us (0.36)
  the two profiles are of different devices: /device:TPU:4 before, /device:TPU:2 now
where the time goes in v1:
time: 145 us
  Pallas kernels  137 us (94%)
  local copies, waits for them, and re-layouts  5.92 us (4%)
    pallas_call x1, Pallas kernels, body(): pl.pallas_call(kernel, out_shape=(jax.ShapeDtypeStruct((TOK, WIDTH), BF16...  137 us
    unnamed x15, local copies, waits for them, and re-layouts  5.34 us

profile of v1, /device:TPU:2, one launch (start us, length us, event | category | flops | bytes accessed | tf_op | source)
XLA Modules:
  0.0 144.6 jit_solution(8320697306923841103)
XLA Ops:
  0.6 0.0 copy-start.4
  0.6 0.6 copy-done.4
  1.3 0.6 dynamic_slice.3.mate_ref
  1.9 0.0 copy-start.5
  1.9 0.0 copy-start.2
  1.9 0.7 copy-done.5
  2.5 0.2 select_reduce_fusion.1
  2.7 0.0 copy-done.2
  2.7 0.1 select_reduce_fusion
  2.8 0.0 copy-start.3
  2.8 0.7 copy-done.3
  3.5 0.6 pad_maximum_fusion.meta_ref
  4.1 137.1 %shard_map.103 = (bf16[128,1024]{1,0:T(8,128)(2,1)}, f32[64,1024]{1,0:T(8,128)}, f32[32,1024]{1,0:T(8,128)}) custom-call(f32[8,128]{1,0:T(8,128)} %pad_maximum_fusion.meta_ref, bf16[128,1024]{1,0:T(8,128)(2,1)} %tok_ref.1, bf16[128,1024]{1,0:T(8,128)(2,1)} %cot_ref.1, bf16[64,1024]{1,0:T(8,128)(2,1)} %bitcast.8, bf16[32,1024]{1,0:T(8,128)(2,1)} %bitcast.10, ...), custom_call_target="tpu_custom_call" | custom-call | tf_op jit(solution)/shard_map/pallas_call | solution.py:474
  141.2 0.0 copy-start
  141.2 1.7 %copy.15 = bf16[128,1024]{1,0:T(8,128)(2,1)} copy(bf16[128,1024]{1,0:T(8,128)(2,1)} %get-tuple-element.12) | data formatting | bytes 524288
  142.9 0.0 copy-done
  142.9 0.0 copy-start.1
  142.9 0.7 copy.16
  143.6 0.3 copy-done.1
  143.9 0.7 copy.17
  (1 shorter events, 0.0 us)
Async XLA Ops:
  0.6 0.7 copy-start.4
  1.9 0.7 copy-start.5
  1.9 0.8 copy-start.2
  2.8 0.7 copy-start.3
  141.2 1.7 %copy-start = (f32[64,1024]{1,0:T(8,128)S(1)}, f32[64,1024]{1,0:T(8,128)}, u32[]{:S(2)}) copy-start(f32[64,1024]{1,0:T(8,128)} %get-tuple-element.7) | copy-start | bytes 786436
  142.9 1.0 copy-start.1

commit v2 on v1

--- a/solution.py
+++ b/solution.py
@@ -21,7 +21,8 @@
 FF = 512
 GU = 64
 DN = 32
-SEMS = 160
+PART = 32
+SEMS = 192
 
 BEHIND = {1: 0, 2: 2, 3: 4, 4: 6, 5: 5, 6: 3, 7: 1}
 AHEAD = {1: 1, 2: 3, 3: 5, 4: 6, 5: 4, 6: 2, 7: 0}
@@ -43,11 +44,11 @@
 
 
 def kernel(
-    meta_ref, tok_ref, cot_ref, gu_ref, dn_ref, mate_ref,
+    ids_ref, gates_ref, tok_ref, cot_ref, gu_ref, dn_ref, placement_ref, partner_ref,
     tg_out, gu_out, dn_out,
     gx, gc, gm, tri, sel, gcol, stx, stu, ex, eu, wgu, wdn, hb, qb, bk, rb,
-    tgp, sz, rz, pgu, pdn, rygu, rydn, txgu, txdn, rxgu, rxdn, slgu, sldn, rlgu, rldn,
-    ssem, rsem,
+    tgp, sz, rz, agu, adn, pgu, pdn, ry, tx, rx, sl, rl, tgb, gub, dnb,
+    ssem, rsem, lsem,
 ):
     dpi = lax.axis_index("dp")
     ei = lax.axis_index("expert")
@@ -72,6 +73,14 @@
     pl.semaphore_wait(barrier, len(peers))
 
     sent = []
+
+    local = []
+
+    def move(src, dst):
+        copy = pltpu.make_async_copy(src, dst, lsem.at[len(local)])
+        copy.start()
+        local.append(copy)
+        return copy
 
     def send(src, dst, device, arrives=None):
         number = len(sent)
@@ -101,7 +110,7 @@
         return ref.at[pl.ds(pl.multiple_of(owner * rows, rows), rows)]
 
     sides = {"own": xl, "oth": 1 - xl}
-    whole = {"gu": (wgu, GU, gu_ref), "dn": (wdn, DN, dn_ref)}
+    whole = {"gu": (wgu, GU, gu_ref.at[0]), "dn": (wdn, DN, dn_ref.at[0])}
     reach = {("own", 1): 4, ("own", -1): 3, ("oth", 1): 3, ("oth", -1): 4}
     coming = {}
 
@@ -142,7 +151,7 @@
         for way, order in ((1, BEHIND), (-1, AHEAD)):
             if hop > 3 and way < 0:
                 continue
-            source = meta_ref if hop == 1 else gm.at[order[hop - 1]]
+            source = gm.at[OWN if hop == 1 else order[hop - 1]]
             ring["m", way, hop] = send(source, gm.at[order[hop]], zdev(way))
 
     def pass_block(name, hop):
@@ -159,15 +168,19 @@
                 source, target = source.at[part], target.at[part]
             ring[name, way, hop] = send(source, target, zdev(way))
 
+    ids = ids_ref[...]
+    holder = jnp.zeros(ids.shape, F32)
+    for e in range(32):
+        holder = jnp.where(ids == e, partner_ref[placement_ref[e]].astype(F32), holder)
+    gm[OWN, 0:4, :] = holder
+    gm[OWN, 4:8, :] = gates_ref[...]
     pass_meta(1)
     pass_block("x", 1)
     pass_block("c", 1)
-
-    gx[OWN * TOK :, :] = tok_ref[...]
-    gc[OWN * TOK :, :] = cot_ref[...]
-    gm[OWN] = meta_ref[...]
+    own_parts = [move(tok_ref, block(gx, OWN)), move(cot_ref, block(gc, OWN))]
     for kind, (buffer, rows, mine) in whole.items():
-        slice_at(buffer, rows, xl, 0)[...] = mine[...]
+        own_parts.append(move(mine, slice_at(buffer, rows, xl, 0)))
+
     before = lax.broadcasted_iota(jnp.int32, (2 * TOK, 2 * TOK), 0)
     after = lax.broadcasted_iota(jnp.int32, (2 * TOK, 2 * TOK), 1)
     same_block = lax.div(before, TOK) == lax.div(after, TOK)
@@ -217,10 +230,12 @@
 
     returned = {}
 
-    def expert(pair):
+    def rows_here(pair):
         for name in ("x", "c"):
             for k in (1, 2, 3):
                 there[name, pair, k].wait_recv()
+
+    def expert(pair):
         rows = slice(pair * ROWS, (pair + 1) * ROWS)
         for tile in range(0, FF, 256):
             cols = pl.ds(tile, 256)
@@ -238,6 +253,8 @@
             value = dot(qb[rows], wgu[cols], LAST_LAST).astype(BF16)
             bk[rows, cols] = value
             rb[pair * ROWS : pair * ROWS + PAIR, cols] = value[:PAIR]
+
+    def give_back(pair):
         for k in (2, 3, 1):
             part = pl.ds((pair * 4 + k) * PAIR, PAIR)
             returned[pair, k] = send(bk.at[part], rb.at[part], plane[k])
@@ -273,63 +290,110 @@
             sums[index, 7].wait_recv()
             cols = slice(index * 512, (index + 1) * 512)
             total = tgp[OWN * TOK :, cols] + rz[index, 6].astype(F32)
-            tg_out[:, cols] = total.astype(BF16)
-
-    partial = {"gu": (pgu, GU, rygu), "dn": (pdn, DN, rydn)}
+            tgb[:, cols] = total.astype(BF16)
+        move(tgb, tg_out)
+
+    parts = {"dn": (pdn, DN, 0, 0), "g0": (pgu, GU, 0, 1), "g1": (pgu, GU, PART, 2)}
     lanes = {("own", 1): 0, ("own", -1): 4, ("oth", 1): 7, ("oth", -1): 10}
     chain = {}
 
-    def grad_step(kind, side, left):
-        buffer, rows, received = partial[kind]
-        for way in (1, -1):
-            if left > reach[side, way]:
-                continue
-            term = slice_at(buffer, rows, sides[side], way * left)
-            if left == reach[side, way]:
-                source = term
-            else:
-                chain[kind, side, way, left + 1].wait_recv()
-                source = received.at[lanes[side, way] + left]
-                source[...] = (source[...].astype(F32) + term[...].astype(F32)).astype(BF16)
-            chain[kind, side, way, left] = send(
-                source, received.at[lanes[side, way] + left - 1], ydev(way)
-            )
+    def part_at(kind, side, delta):
+        buffer, rows, first, _ = parts[kind]
+        owner = sides[side] * NY + lax.rem(y + delta + NY, NY)
+        return buffer.at[pl.ds(pl.multiple_of(owner * rows + first, PART), PART)]
+
+    def grad_step(kind, side, way, left):
+        received = ry.at[parts[kind][3]]
+        term = part_at(kind, side, way * left)
+        if left == reach[side, way]:
+            source = term
+        else:
+            chain[kind, side, way, left + 1].wait_recv()
+            source = received.at[lanes[side, way] + left]
+            source[...] = (source[...].astype(F32) + term[...].astype(F32)).astype(BF16)
+        chain[kind, side, way, left] = send(
+            source, received.at[lanes[side, way] + left - 1], ydev(way)
+        )
+
+    def grad_round(kind, number):
+        if number == 1:
+            grad_step(kind, "oth", 1, 3)
+            grad_step(kind, "oth", -1, 4)
+            grad_step(kind, "own", 1, 4)
+            grad_step(kind, "own", -1, 3)
+        elif number == 2:
+            grad_step(kind, "oth", 1, 2)
+            grad_step(kind, "oth", -1, 3)
+            grad_step(kind, "own", 1, 3)
+            grad_step(kind, "own", -1, 2)
+        elif number == 3:
+            grad_step(kind, "oth", 1, 1)
+            grad_step(kind, "oth", -1, 2)
+            grad_step(kind, "own", 1, 2)
+            grad_step(kind, "own", -1, 1)
+        else:
+            grad_step(kind, "oth", -1, 1)
+            grad_step(kind, "own", 1, 1)
 
     def grad_sum(kind, side):
-        buffer, rows, received = partial[kind]
-        total = slice_at(buffer, rows, sides[side], 0)[...].astype(F32)
+        total = part_at(kind, side, 0)[...].astype(F32)
         for way in (1, -1):
             chain[kind, side, way, 1].wait_recv()
-            total = total + received[lanes[side, way]].astype(F32)
+            total = total + ry[parts[kind][3], lanes[side, way]].astype(F32)
         return total
 
-    crossing = {"gu": (txgu, rxgu), "dn": (txdn, rxdn)}
-    swaps = {"gu": (slgu, rlgu, gu_out), "dn": (sldn, rldn, dn_out)}
+    results = {"dn": (dnb, dn_out, 0), "g0": (gub, gu_out, 0), "g1": (gub, gu_out, PART)}
     crossed, moved = {}, {}
 
     def grad_cross(kind):
-        outgoing, incoming = crossing[kind]
-        outgoing[...] = grad_sum(kind, "oth").astype(BF16)
-        crossed[kind] = send(outgoing, incoming, other_side)
+        index = parts[kind][3]
+        tx[index] = grad_sum(kind, "oth").astype(BF16)
+        crossed[kind] = send(tx.at[index], rx.at[index], other_side)
 
     def grad_swap(kind):
-        staged, landed, out = swaps[kind]
+        index = parts[kind][3]
+        kept, _, first = results[kind]
         total = grad_sum(kind, "own")
         crossed[kind].wait_recv()
-        total = total + crossing[kind][1][...].astype(F32)
-        out[...] = total
-        staged[...] = total.astype(BF16)
+        total = total + rx[index].astype(F32)
+        kept[first : first + PART, :] = total
+        sl[index] = total.astype(BF16)
         for bit in (4, 3, 2, 1, 0):
-            moved[kind, bit] = send(staged, landed.at[bit], mates[bit])
+            moved[kind, bit] = send(sl.at[index], rl.at[index, bit], mates[bit])
 
     def grad_last(kind):
-        _, landed, out = swaps[kind]
-        mate = mate_ref[0]
-        value = out[...]
+        kept, out, first = results[kind]
+        mate = partner_ref[ei]
+        value = kept[first : first + PART, :]
         for bit in range(5):
             moved[kind, bit].wait_recv()
-            value = jnp.where(mate == flip(ei, bit), landed[bit].astype(F32), value)
-        out[...] = value
+            landed = rl[parts[kind][3], bit].astype(F32)
+            value = jnp.where(mate == flip(ei, bit), landed, value)
+        kept[first : first + PART, :] = value
+        rows = pl.ds(first, PART)
+        move(kept.at[rows], out.at[rows])
+
+    early = 3 * ROWS
+
+    def ahead_of_last():
+        for tile in range(0, FF, 256):
+            cols = pl.ds(tile, 256)
+            adn[cols, :] = dot(hb[0:early, cols], eu[0:early], FIRST_FIRST)
+        for tile in range(0, WIDTH, 256):
+            cols = pl.ds(tile, 256)
+            agu[cols, :] = dot(ex[0:early, cols], qb[0:early], FIRST_FIRST)
+
+    def last_dn():
+        for tile in range(0, FF, 256):
+            cols = pl.ds(tile, 256)
+            term = dot(hb[early:, cols], eu[early:], FIRST_FIRST)
+            pdn[cols, :] = (adn[cols, :] + term).astype(BF16)
+
+    def last_gu():
+        for tile in range(0, WIDTH, 256):
+            cols = pl.ds(tile, 256)
+            term = dot(ex[early:, cols], qb[early:], FIRST_FIRST)
+            pgu[cols, :] = (agu[cols, :] + term).astype(BF16)
 
     def arrive_side():
         for kind in whole:
@@ -359,78 +423,93 @@
     pass_block("x", 4)
     choose(2)
     dispatch("x", 2)
+    ring["m", 1, 4].wait_recv()
+    choose(3)
+    for copy in own_parts:
+        copy.wait()
+    pass_block("c", 4)
+    dispatch("c", 2)
     last_weights("own")
     last_weights("oth")
-    ring["m", 1, 4].wait_recv()
-    choose(3)
-    pass_block("c", 4)
-    dispatch("c", 2)
+    rows_here(0)
     expert(0)
     for way in (1, -1):
         ring["x", way, 4].wait_recv()
     dispatch("x", 3)
+    rows_here(1)
+    expert(1)
     for way in (1, -1):
         ring["c", way, 4].wait_recv()
     dispatch("c", 3)
-    expert(1)
+    rows_here(2)
     expert(2)
+    ahead_of_last()
+    rows_here(3)
+    give_back(0)
+    give_back(1)
+    expert(3)
+    last_dn()
+    grad_round("dn", 1)
+    last_gu()
+    grad_round("g0", 1)
+    give_back(2)
+    give_back(3)
     combine(0)
     token_step(1)
+    grad_round("dn", 2)
+    grad_round("g0", 2)
     combine(1)
     token_step(2)
-    expert(3)
-    for tile in range(0, FF, 256):
-        cols = pl.ds(tile, 256)
-        pdn[cols, :] = dot(hb[:, cols], eu[...], FIRST_FIRST).astype(BF16)
-    grad_step("dn", "oth", 4)
-    grad_step("dn", "own", 4)
-    grad_step("dn", "oth", 3)
-    grad_step("dn", "own", 3)
-    for tile in range(0, WIDTH, 256):
-        cols = pl.ds(tile, 256)
-        pgu[cols, :] = dot(ex[:, cols], qb[...], FIRST_FIRST).astype(BF16)
-    grad_step("gu", "oth", 4)
-    grad_step("gu", "own", 4)
-    grad_step("gu", "oth", 3)
-    grad_step("gu", "own", 3)
+    grad_round("dn", 3)
+    grad_round("g1", 1)
     combine(2)
     token_step(3)
+    grad_round("dn", 4)
+    grad_round("g0", 3)
     combine(3)
     token_step(4)
-    grad_step("dn", "oth", 2)
-    grad_step("dn", "own", 2)
+    grad_cross("dn")
+    grad_round("g1", 2)
     token_step(5)
-    grad_step("gu", "oth", 2)
-    grad_step("gu", "own", 2)
+    grad_round("g0", 4)
+    grad_swap("dn")
     token_step(6)
-    grad_step("dn", "oth", 1)
-    grad_step("dn", "own", 1)
+    grad_round("g1", 3)
+    grad_cross("g0")
     token_step(7)
-    grad_step("gu", "oth", 1)
-    grad_step("gu", "own", 1)
+    grad_round("g1", 4)
+    grad_swap("g0")
+    grad_cross("g1")
     token_last()
-    grad_cross("dn")
-    grad_swap("dn")
-    grad_cross("gu")
-    grad_swap("gu")
+    grad_swap("g1")
     grad_last("dn")
-    grad_last("gu")
+    grad_last("g0")
+    grad_last("g1")
+    for copy in local[len(own_parts) :]:
+        copy.wait()
     for copy in sent:
         copy.wait_send()
     assert len(sent) <= SEMS
 
 
-def table_lookup(keys, table):
-    hits = keys[..., None] == jnp.arange(table.shape[0], dtype=jnp.int32)
-    return jnp.sum(jnp.where(hits, table, 0), axis=-1)
+def hand_on(*refs):
+    count = len(refs) // 3
+    sources, results, held = refs[:count], refs[count : 2 * count], refs[2 * count : 3 * count]
+    arriving, leaving = refs[3 * count :]
+    copies = []
+    for index in range(count):
+        copies.append(pltpu.make_async_copy(sources[index], held[index], arriving.at[index]))
+        copies[index].start()
+    for index in range(count):
+        copies[index].wait()
+        target = results[index] if index == 0 else results[index].at[0]
+        copies[index] = pltpu.make_async_copy(held[index], target, leaving.at[index])
+        copies[index].start()
+    for copy in copies:
+        copy.wait()
 
 
 def body(tokens, cotangent, gates, expert_ids, placement, partner, w_gate_up, w_down):
-    here = lax.axis_index("expert")
-    mate = lax.dynamic_slice_in_dim(partner, here, 1)
-    holder = table_lookup(expert_ids, table_lookup(placement, partner))
-    meta = jnp.concatenate([holder.astype(F32).T, gates.T], axis=0)
-
     def vmem(*shape, dtype=BF16):
         return pltpu.VMEM(shape, dtype)
 
@@ -455,37 +534,57 @@
         vmem(NZ * TOK, WIDTH, dtype=F32),
         vmem(2, TOK, 512),
         vmem(2, 7, TOK, 512),
+        vmem(WIDTH, 2 * FF, dtype=F32),
+        vmem(FF, WIDTH, dtype=F32),
         vmem(WIDTH, 2 * FF),
         vmem(FF, WIDTH),
-        vmem(14, GU, 2 * FF),
-        vmem(14, DN, WIDTH),
-        vmem(GU, 2 * FF),
-        vmem(DN, WIDTH),
-        vmem(GU, 2 * FF),
-        vmem(DN, WIDTH),
-        vmem(GU, 2 * FF),
-        vmem(DN, WIDTH),
-        vmem(5, GU, 2 * FF),
-        vmem(5, DN, WIDTH),
+        vmem(3, 14, PART, WIDTH),
+        vmem(3, PART, WIDTH),
+        vmem(3, PART, WIDTH),
+        vmem(3, PART, WIDTH),
+        vmem(3, 5, PART, WIDTH),
+        vmem(TOK, WIDTH),
+        vmem(GU, 2 * FF, dtype=F32),
+        vmem(DN, WIDTH, dtype=F32),
         pltpu.SemaphoreType.DMA((SEMS,)),
         pltpu.SemaphoreType.DMA((SEMS,)),
+        pltpu.SemaphoreType.DMA((8,)),
     ]
     in_vmem = pl.BlockSpec(memory_space=pltpu.VMEM)
-    token_grad, grad_gu, grad_dn = pl.pallas_call(
+    in_smem = pl.BlockSpec(memory_space=pltpu.SMEM)
+    anywhere = pl.BlockSpec(memory_space=pl.ANY)
+    results = pl.pallas_call(
         kernel,
         out_shape=(
             jax.ShapeDtypeStruct((TOK, WIDTH), BF16),
             jax.ShapeDtypeStruct((GU, 2 * FF), F32),
             jax.ShapeDtypeStruct((DN, WIDTH), F32),
         ),
-        in_specs=[in_vmem] * 5 + [pl.BlockSpec(memory_space=pltpu.SMEM)],
-        out_specs=(in_vmem,) * 3,
+        in_specs=[in_vmem] * 2 + [anywhere] * 4 + [in_smem] * 2,
+        out_specs=(anywhere,) * 3,
         scratch_shapes=scratch,
         compiler_params=pltpu.CompilerParams(
-            collective_id=0, has_side_effects=True, vmem_limit_bytes=56 * 1024 * 1024
+            collective_id=0, has_side_effects=True, vmem_limit_bytes=58 * 1024 * 1024
         ),
-    )(meta, tokens, cotangent, w_gate_up[0], w_down[0], mate)
-    return token_grad, grad_gu[None], grad_dn[None]
+    )(expert_ids.T, gates.T, tokens, cotangent, w_gate_up, w_down, placement, partner)
+    return pl.pallas_call(
+        hand_on,
+        out_shape=(
+            jax.ShapeDtypeStruct((TOK, WIDTH), BF16),
+            jax.ShapeDtypeStruct((1, GU, 2 * FF), F32),
+            jax.ShapeDtypeStruct((1, DN, WIDTH), F32),
+        ),
+        in_specs=[anywhere] * 3,
+        out_specs=(anywhere,) * 3,
+        scratch_shapes=[
+            vmem(TOK, WIDTH),
+            vmem(GU, 2 * FF, dtype=F32),
+            vmem(DN, WIDTH, dtype=F32),
+            pltpu.SemaphoreType.DMA((3,)),
+            pltpu.SemaphoreType.DMA((3,)),
+        ],
+        compiler_params=pltpu.CompilerParams(vmem_limit_bytes=58 * 1024 * 1024),
+    )(*results)
 
 
 def solution(mesh):

time: 145 us -> 125 us (0.86)
  the two profiles are of different devices: /device:TPU:2 before, /device:TPU:152 now
where the time goes in v2:
time: 125 us
  Pallas kernels  124 us (99%)
    pallas_call x1, Pallas kernels, body(): pl.pallas_call(kernel, out_shape=(jax.ShapeDtypeStruct((TOK, WIDTH), BF16...  123 us

profile of v2, /device:TPU:152, one launch (start us, length us, event | category | flops | bytes accessed | tf_op | source)
XLA Modules:
  0.0 125.1 jit_solution(9330539056098643272)
XLA Ops:
  0.6 122.6 %shard_map.103 = (bf16[128,1024]{1,0:T(8,128)(2,1)}, f32[64,1024]{1,0:T(8,128)}, f32[32,1024]{1,0:T(8,128)}) custom-call(s32[4,128]{1,0:T(4,128)} %bitcast.2, f32[4,128]{1,0:T(4,128)} %bitcast.3, bf16[128,1024]{1,0:T(8,128)(2,1)} %tok_ref.1, bf16[128,1024]{1,0:T(8,128)(2,1)} %cot_ref.1, bf16[1,64,1024]{2,1,0:T(8,128)(2,1)} %gu_ref.1, ...), custom_call_target="tpu_custom_call" | custom-call | tf_op jit(solution)/shard_map/pallas_call | solution.py:556
  123.3 1.8 %shard_map.104 = (bf16[128,1024]{1,0:T(8,128)(2,1)}, f32[1,64,1024]{2,1,0:T(8,128)}, f32[1,32,1024]{2,1,0:T(8,128)}) custom-call(bf16[128,1024]{1,0:T(8,128)(2,1)} %get-tuple-element.6.refs_0_, f32[64,1024]{1,0:T(8,128)} %get-tuple-element.7.refs_1_, f32[32,1024]{1,0:T(8,128)} %get-tuple-element.8.refs_2_), custom_call_target="tpu_custom_call" | custom-call | tf_op jit(solution)/shard_map/pallas_call | solution.py:570

commit v3 on v2

v3 whole, which is shorter than its diff:
```python
import math

import jax
import jax.numpy as jnp
from jax import lax
from jax.experimental import pallas as pl
from jax.experimental.pallas import tpu as pltpu
from jax.sharding import PartitionSpec as P

MESH = pl.DeviceIdType.MESH
BF16 = jnp.bfloat16
F32 = jnp.float32

NZ = 8
NY = 8
CAP = 24
PAIR = 2 * CAP
ROWS = 4 * PAIR
TOK = 128
WIDTH = 1024
FF = 512
GU = 64
DN = 32
PARTS = (32, 32, 32)
RECEIVES = 89
GROUPS = ("weights", "meta", "ring", "out", "back", "sums", "grads", "swap", "pieces")

BEHIND = {1: 0, 2: 2, 3: 4, 4: 6, 5: 5, 6: 3, 7: 1}
AHEAD = {1: 1, 2: 3, 3: 5, 4: 6, 5: 4, 6: 2, 7: 0}
OPPOSITE, OWN = 6, 7


def flip(value, bit):
    size = 1 << bit
    return value + size - 2 * size * (lax.rem(lax.div(value, size), 2))


def dot(a, b, dims):
    return lax.dot_general(a, b, (dims, ((), ())), preferred_element_type=F32)


ROWS_COLS = ((1,), (0,))
LAST_LAST = ((1,), (1,))
FIRST_FIRST = ((0,), (0,))


def kernel(
    ids_ref, gates_ref, tok_ref, cot_ref, gu_ref, dn_ref, placement_ref, partner_ref,
    tg_out, gu_out, dn_out,
    gx, gc, gm, tri, sel, gcol, stx, stu, ex, eu, wgu, wdn, hb, qb, bk, rb,
    tgp, sz, rz, agu, adn, pgu, pdn, ry, tx, rx, sl, rl, cut, via, onward, whence, tgb, gub, dnb,
    ssem, rsem, lsem,
):
    dpi = lax.axis_index("dp")
    ei = lax.axis_index("expert")
    xl, y = lax.div(dpi, NY), lax.rem(dpi, NY)
    z, c = lax.div(ei, 4), lax.rem(ei, 4)

    def ydev(delta):
        return (xl * NY + lax.rem(y + delta + NY, NY), ei)

    def zdev(delta):
        return (dpi, lax.rem(z + delta + NZ, NZ) * 4 + c)

    column = [c, flip(c, 0), flip(c, 1), flip(flip(c, 0), 1)]
    plane = [(dpi, z * 4 + q) for q in column]
    other_side = ((1 - xl) * NY + y, ei)

    barrier = pltpu.get_barrier_semaphore()
    peers = [zdev(r) for r in range(1, NZ)] + plane[1:] + [ydev(1), ydev(-1), other_side]
    for peer in peers:
        pl.semaphore_signal(barrier, inc=1, device_id=peer, device_id_type=MESH)
    pl.semaphore_wait(barrier, len(peers))

    sent = {group: [] for group in GROUPS}
    receives = []

    local = []

    def move(src, dst):
        copy = pltpu.make_async_copy(src, dst, lsem.at[len(local)])
        copy.start()
        local.append(copy)
        return copy

    def new():
        receives.append(len(receives))
        return receives[-1]

    def send(group, receive, src, dst, device):
        copy = pltpu.make_async_remote_copy(
            src_ref=src,
            dst_ref=dst,
            send_sem=ssem.at[GROUPS.index(group)],
            recv_sem=rsem.at[receive],
            device_id=device,
            device_id_type=MESH,
        )
        copy.start()
        sent[group].append(src)

    def arrive(receive, ref):
        pltpu.make_async_remote_copy(
            src_ref=ref,
            dst_ref=ref,
            send_sem=ssem.at[0],
            recv_sem=rsem.at[receive],
            device_id=other_side,
            device_id_type=MESH,
        ).wait_recv()

    def slice_at(ref, rows, side, delta):
        owner = side * NY + lax.rem(y + delta + NY, NY)
        return ref.at[pl.ds(pl.multiple_of(owner * rows, rows), rows)]

    sides = {"own": xl, "oth": 1 - xl}
    whole = {"gu": (wgu, GU, gu_ref.at[0]), "dn": (wdn, DN, dn_ref.at[0])}
    reach = {("own", 1): 4, ("own", -1): 3, ("oth", 1): 3, ("oth", -1): 4}
    coming = {}
    one_slice = wgu.at[pl.ds(0, GU + DN)]

    def pass_weights(side, hop):
        for way in (1, -1):
            if hop > reach[side, way]:
                continue
            if hop > 1:
                arrive(coming[side, way, hop - 1], one_slice)
            coming[side, way, hop] = new()
            for buffer, rows, mine in whole.values():
                target = slice_at(buffer, rows, sides[side], -way * (hop - 1))
                source = mine if hop == 1 and side == "own" else target
                send("weights", coming[side, way, hop], source, target, ydev(way))

    def last_weights(side):
        for way in (1, -1):
            arrive(coming[side, way, reach[side, way]], one_slice)

    across = new()
    for buffer, rows, mine in whole.values():
        send("weights", across, mine, slice_at(buffer, rows, xl, 0), other_side)
    pass_weights("own", 1)

    def block(ref, index):
        return ref.at[pl.ds(index * TOK, TOK)]

    ring = {}

    def pass_meta(hop):
        if hop > 1:
            arrive(ring["m", hop - 1], gm.at[pl.ds(2 * hop - 4, 2)])
        ring["m", hop] = new()
        for way, order in ((1, BEHIND), (-1, AHEAD)):
            if hop > 3 and way < 0:
                continue
            source = gm.at[OWN if hop == 1 else order[hop - 1]]
            send("meta", ring["m", hop], source, gm.at[order[hop]], zdev(way))

    def block_here(name, hop):
        buffer = gx if name == "x" else gc
        arrive(ring[name, hop], buffer.at[pl.ds(2 * (hop - 1) * TOK, TOK if hop == 4 else 2 * TOK)])

    def pass_block(name, hop):
        mine, buffer = {"x": (tok_ref, gx), "c": (cot_ref, gc)}[name]
        if hop > 1:
            block_here(name, hop - 1)
        half = TOK // 2
        ring[name, hop] = new()
        for way, order in ((1, BEHIND), (-1, AHEAD)):
            source = mine if hop == 1 else block(buffer, order[hop - 1])
            target = block(buffer, order[hop])
            if hop == 4:
                part = pl.ds(0 if way > 0 else half, half)
                source, target = source.at[part], target.at[part]
            send("ring", ring[name, hop], source, target, zdev(way))

    ids = ids_ref[...]
    holder = jnp.zeros(ids.shape, F32)
    for e in range(32):
        holder = jnp.where(ids == e, partner_ref[placement_ref[e]].astype(F32), holder)
    gm[OWN, 0:4, :] = holder
    gm[OWN, 4:8, :] = gates_ref[...]
    pass_meta(1)
    pass_block("x", 1)
    pass_block("c", 1)
    own_parts = [move(tok_ref, block(gx, OWN)), move(cot_ref, block(gc, OWN))]
    for buffer, rows, mine in whole.values():
        own_parts.append(move(mine, slice_at(buffer, rows, xl, 0)))

    before = lax.broadcasted_iota(jnp.int32, (2 * TOK, 2 * TOK), 0)
    after = lax.broadcasted_iota(jnp.int32, (2 * TOK, 2 * TOK), 1)
    same_block = lax.div(before, TOK) == lax.div(after, TOK)
    tri[...] = jnp.where(same_block & (before < after), 1.0, 0.0).astype(BF16)

    def choose(pair):
        both = jnp.concatenate([gm[2 * pair], gm[2 * pair + 1]], axis=1)
        named, weight = both[0:4], both[4:8]
        hits, scales = [], []
        for q in column:
            hit = jnp.where(named == (z * 4 + q).astype(F32), 1.0, 0.0)
            hits.append(jnp.sum(hit, axis=0, keepdims=True))
            scales.append(jnp.sum(hit * weight, axis=0, keepdims=True))
        marks = jnp.concatenate(hits + [jnp.zeros((12, 2 * TOK), F32)], axis=0)
        ranks = dot(marks.astype(BF16), tri[...], ROWS_COLS)
        slot = lax.broadcasted_iota(jnp.int32, (CAP, 2 * TOK), 0).astype(F32)
        lane = lax.broadcasted_iota(jnp.int32, (CAP, 2 * TOK), 1)
        parts, columns = [], []
        for k in range(4):
            found = (ranks[k : k + 1] == slot) & (hits[k] > 0.5)
            for half in range(2):
                here = lane < TOK if half == 0 else lane >= TOK
                part = jnp.where(found & here, 1.0, 0.0)
                parts.append(part)
                columns.append(jnp.sum(part * scales[k], axis=1, keepdims=True))
        sel[pair] = jnp.concatenate(parts, axis=0).astype(BF16)
        gcol[pair] = jnp.broadcast_to(jnp.concatenate(columns, axis=0), (ROWS, 128))

    there = {}

    def dispatch(name, pair):
        buffer, staged, arrived = {"x": (gx, stx, ex), "c": (gc, stu, eu)}[name]
        for tile in range(0, WIDTH, 512):
            cols = pl.ds(tile, 512)
            rows = dot(sel[pair], buffer[2 * pair * TOK : 2 * (pair + 1) * TOK, cols], ROWS_COLS)
            if name == "c":
                rows = gcol[pair][:, 0:1] * rows
            rows = rows.astype(BF16)
            arrived[pair * ROWS : pair * ROWS + PAIR, cols] = rows[:PAIR]
            staged[pair * 3 * PAIR : (pair + 1) * 3 * PAIR, cols] = rows[PAIR:]
        there[name, pair] = new()
        for k in (2, 3, 1):
            send(
                "out",
                there[name, pair],
                staged.at[pl.ds((pair * 3 + k - 1) * PAIR, PAIR)],
                arrived.at[pl.ds((pair * 4 + k) * PAIR, PAIR)],
                plane[k],
            )

    returned = {}

    def from_others(ref, pair):
        return ref.at[pl.ds(pair * ROWS + PAIR, 3 * PAIR)]

    def rows_here(pair):
        arrive(there["x", pair], from_others(ex, pair))
        arrive(there["c", pair], from_others(eu, pair))

    def expert(pair):
        rows = slice(pair * ROWS, (pair + 1) * ROWS)
        for tile in range(0, FF, 256):
            cols = pl.ds(tile, 256)
            up_cols = pl.ds(FF + tile, 256)
            a = dot(ex[rows], wgu[:, cols], ROWS_COLS)
            b = dot(ex[rows], wgu[:, up_cols], ROWS_COLS)
            dh = dot(eu[rows], wdn[cols], LAST_LAST)
            s = jax.nn.sigmoid(a)
            active = a * s
            hb[rows, cols] = (active * b).astype(BF16)
            qb[rows, cols] = (dh * b * (s * (1.0 + a * (1.0 - s)))).astype(BF16)
            qb[rows, up_cols] = (dh * active).astype(BF16)
        for tile in range(0, WIDTH, 256):
            cols = pl.ds(tile, 256)
            value = dot(qb[rows], wgu[cols], LAST_LAST).astype(BF16)
            bk[rows, cols] = value
            rb[pair * ROWS : pair * ROWS + PAIR, cols] = value[:PAIR]

    def give_back(pair):
        returned[pair] = new()
        for k in (2, 3, 1):
            part = pl.ds((pair * 4 + k) * PAIR, PAIR)
            send("back", returned[pair], bk.at[part], rb.at[part], plane[k])

    def combine(pair):
        arrive(returned[pair], from_others(rb, pair))
        for tile in range(0, WIDTH, 512):
            cols = pl.ds(tile, 512)
            tgp[pair * 256 : (pair + 1) * 256, cols] = dot(
                sel[pair], rb[pair * ROWS : (pair + 1) * ROWS, cols], FIRST_FIRST
            )

    ways = ((0, 1, BEHIND), (1, -1, AHEAD))
    sums = {}

    def token_step(step, half):
        if step > 1:
            arrive(sums[step - 1, half], rz.at[step - 2, half])
        sums[step, half] = new()
        for index, way, order in ways:
            start, low = order[step] * TOK, index * 512 + half * 256
            term = tgp[start : start + TOK, low : low + 256]
            if step == 1:
                sz[half, index] = term.astype(BF16)
                source = sz.at[half, index]
            else:
                source = rz.at[step - 2, half, index]
                source[...] = (source[...].astype(F32) + term).astype(BF16)
            send("sums", sums[step, half], source, rz.at[step - 1, half, index], zdev(way))

    def token_last():
        for half in range(2):
            arrive(sums[7, half], rz.at[6, half])
            for index, _, _ in ways:
                low = index * 512 + half * 256
                total = tgp[OWN * TOK :, low : low + 256] + rz[6, half, index].astype(F32)
                tgb[:, low : low + 256] = total.astype(BF16)
        move(tgb, tg_out)

    parts = {"dn": (pdn, 0, PARTS[0]), "g0": (pgu, 0, PARTS[1]), "g1": (pgu, 32, PARTS[2])}
    kinds = list(parts)
    both = ("oth", "own")
    chain = {}

    def part_at(kind, side, delta):
        buffer, low, rows = parts[kind]
        return buffer.at[sides[side] * NY + lax.rem(y + delta + NY, NY), pl.ds(low, rows)]

    def grad_here(kind, side, number):
        received = ry[kinds.index(kind)].at[both.index(side), number - 1]
        if number == 4:
            received = received.at[0 if reach[side, 1] == 4 else 1]
        arrive(chain[kind, side, number], received)

    def grad_round(kind, side, number):
        received = ry[kinds.index(kind)].at[both.index(side)]
        if number > 1:
            grad_here(kind, side, number - 1)
        chain[kind, side, number] = new()
        for slot, way in ((0, 1), (1, -1)):
            left = reach[side, way] + 1 - number
            if left < 1:
                continue
            source = part_at(kind, side, way * left)
            if number > 1:
                term = source[...].astype(F32)
                source = received.at[number - 2, slot]
                source[...] = (source[...].astype(F32) + term).astype(BF16)
            target = received.at[number - 1, slot]
            send("grads", chain[kind, side, number], source, target, ydev(way))

    def grad_sum(kind, side):
        grad_here(kind, side, 4)
        total = part_at(kind, side, 0)[...].astype(F32)
        for slot, way in ((0, 1), (1, -1)):
            landed = ry[kinds.index(kind)][both.index(side), reach[side, way] - 1, slot]
            total = total + landed.astype(F32)
        return total

    results = {"dn": (dnb, dn_out, 0), "g0": (gub, gu_out, 0), "g1": (gub, gu_out, 32)}
    crossed, moved, spread, reached = {}, {}, {}, {}

    def grad_cross(kind):
        index = kinds.index(kind)
        tx[index][...] = grad_sum(kind, "oth").astype(BF16)
        crossed[kind] = new()
        send("swap", crossed[kind], tx[index], rx[index], other_side)

    def grad_swap(kind):
        index = kinds.index(kind)
        kept, _, start = results[kind]
        total = grad_sum(kind, "own")
        arrive(crossed[kind], rx[index])
        total = total + rx[index][...].astype(F32)
        kept[start : start + PARTS[index], :] = total
        total = total.astype(BF16)
        sl[index][...] = total
        for piece in range(NZ):
            cut[index][piece] = total[:, piece * 128 : (piece + 1) * 128]
        via[index][0] = cut[index][z]
        spread[kind], moved[kind] = new(), new()
        for r in range(1, NZ):
            source = cut[index].at[lax.rem(z + r, NZ)]
            send("pieces", spread[kind], source, via[index].at[r], zdev(r))
        for bit in (1, 0):
            send("swap", moved[kind], sl[index], rl[index].at[bit], plane[1 << bit])

    def grad_swap_on(kind):
        index = kinds.index(kind)
        arrive(spread[kind], via[index].at[pl.ds(1, NZ - 1)])
        reached[kind] = new()
        for r in range(NZ):
            taker = lax.rem(z + r, NZ)
            giver = lax.div(partner_ref[taker * 4 + c], 4)
            behind = lax.rem(z - giver + NZ, NZ)
            piece = via[index][0]
            for k in range(1, NZ):
                piece = jnp.where(behind == k, via[index][k], piece)
            if r == 0:
                whence[index][z] = piece
                continue
            onward[index][r] = piece
            send("pieces", reached[kind], onward[index].at[r], whence[index].at[z], zdev(r))

    def grad_last(kind):
        index = kinds.index(kind)
        kept, out, start = results[kind]
        mate = partner_ref[ei]
        arrive(moved[kind], rl[index])
        arrive(reached[kind], whence[index].at[pl.ds(1, NZ - 1)])
        value = kept[start : start + PARTS[index], :]
        for bit in range(2):
            value = jnp.where(mate == flip(ei, bit), rl[index][bit].astype(F32), value)
        pieces = [whence[index][piece].astype(F32) for piece in range(NZ)]
        value = jnp.where(lax.div(mate, 4) == z, value, jnp.concatenate(pieces, axis=1))
        kept[start : start + PARTS[index], :] = value
        place = pl.ds(start, PARTS[index])
        move(kept.at[place], out.at[place])

    early = 3 * ROWS

    def ahead_of_last():
        for tile in range(0, FF, 256):
            cols = pl.ds(tile, 256)
            adn[cols, :] = dot(hb[0:early, cols], eu[0:early], FIRST_FIRST)
        for tile in range(0, WIDTH, 256):
            cols = pl.ds(tile, 256)
            agu[cols, :] = dot(ex[0:early, cols], qb[0:early], FIRST_FIRST)

    def last_dn():
        for tile in range(0, FF, 256):
            cols = pl.ds(tile, 256)
            term = dot(hb[early:, cols], eu[early:], FIRST_FIRST)
            total = (adn[cols, :] + term).astype(BF16)
            pdn[tile // DN : (tile + 256) // DN] = total.reshape(256 // DN, DN, WIDTH)

    def last_gu():
        for tile in range(0, WIDTH, 256):
            cols = pl.ds(tile, 256)
            term = dot(ex[early:, cols], qb[early:], FIRST_FIRST)
            total = (agu[cols, :] + term).astype(BF16)
            pgu[tile // GU : (tile + 256) // GU] = total.reshape(256 // GU, GU, 2 * FF)

    arrive(across, one_slice)
    pass_weights("oth", 1)
    pass_weights("own", 2)
    pass_meta(2)
    pass_block("x", 2)
    choose(0)
    dispatch("x", 0)
    pass_weights("oth", 2)
    pass_block("c", 2)
    dispatch("c", 0)
    pass_weights("own", 3)
    pass_meta(3)
    pass_block("x", 3)
    choose(1)
    dispatch("x", 1)
    pass_weights("oth", 3)
    pass_block("c", 3)
    dispatch("c", 1)
    pass_weights("own", 4)
    pass_weights("oth", 4)
    pass_meta(4)
    pass_block("x", 4)
    choose(2)
    dispatch("x", 2)
    arrive(ring["m", 4], gm.at[OPPOSITE])
    choose(3)
    for copy in own_parts:
        copy.wait()
    pass_block("c", 4)
    dispatch("c", 2)
    last_weights("own")
    last_weights("oth")
    rows_here(0)
    expert(0)
    block_here("x", 4)
    dispatch("x", 3)
    rows_here(1)
    expert(1)
    block_here("c", 4)
    dispatch("c", 3)
    rows_here(2)
    expert(2)
    ahead_of_last()
    rows_here(3)
    give_back(0)
    expert(3)
    last_dn()
    grad_round("dn", "own", 1)
    last_gu()
    grad_round("g0", "oth", 1)
    give_back(1)
    grad_round("g1", "oth", 1)
    grad_round("dn", "oth", 1)
    combine(0)
    grad_round("dn", "own", 2)
    give_back(2)
    token_step(1, 1)
    grad_round("g1", "oth", 2)
    grad_round("g1", "own", 1)
    token_step(1, 0)
    combine(1)
    grad_round("dn", "oth", 2)
    token_step(2, 1)
    grad_round("dn", "own", 3)
    token_step(2, 0)
    grad_round("g0", "own", 1)
    give_back(3)
    combine(2)
    grad_round("dn", "oth", 3)
    grad_round("g1", "own", 2)
    token_step(3, 1)
    token_step(3, 0)
    grad_round("g0", "oth", 2)
    grad_round("g1", "oth", 3)
    grad_round("dn", "oth", 4)
    combine(3)
    token_step(4, 1)
    token_step(4, 0)
    grad_round("g0", "own", 2)
    grad_round("g0", "oth", 3)
    token_step(5, 1)
    grad_round("g1", "own", 3)
    grad_cross("dn")
    grad_round("g1", "oth", 4)
    grad_round("dn", "own", 4)
    token_step(5, 0)
    grad_round("g0", "own", 3)
    token_step(6, 1)
    grad_round("g0", "oth", 4)
    token_step(6, 0)
    grad_swap("dn")
    grad_cross("g1")
    token_step(7, 1)
    grad_round("g1", "own", 4)
    grad_round("g0", "own", 4)
    grad_cross("g0")
    token_step(7, 0)
    grad_swap("g1")
    grad_swap("g0")
    grad_swap_on("dn")
    token_last()
    grad_swap_on("g1")
    grad_swap_on("g0")
    grad_last("dn")
    grad_last("g1")
    grad_last("g0")
    for copy in local[len(own_parts) :]:
        copy.wait()
    for group, sources in sent.items():
        size = sum(math.prod(source.shape) for source in sources)
        if group == "meta":
            whole_group = gm.at[pl.ds(0, size // (8 * TOK))]
        elif group == "pieces":
            whole_group = hb.at[pl.ds(0, size // FF)]
        else:
            whole_group = agu.at[pl.ds(0, size // (2 * WIDTH))]
        pltpu.make_async_remote_copy(
            src_ref=whole_group,
            dst_ref=whole_group,
            send_sem=ssem.at[GROUPS.index(group)],
            recv_sem=rsem.at[0],
            device_id=other_side,
            device_id_type=MESH,
        ).wait_send()
    assert len(receives) <= RECEIVES


def hand_on(*refs):
    count = len(refs) // 2
    sources, results, sem = refs[:count], refs[count:-1], refs[-1]
    copies = []
    for index in range(count):
        target = results[index] if index == 0 else results[index].at[0]
        copies.append(pltpu.make_async_copy(sources[index], target, sem.at[index]))
        copies[index].start()
    for copy in copies:
        copy.wait()


def body(tokens, cotangent, gates, expert_ids, placement, partner, w_gate_up, w_down):
    def vmem(*shape, dtype=BF16):
        return pltpu.VMEM(shape, dtype)

    slots = 4 * ROWS
    scratch = [
        vmem(NZ * TOK, WIDTH),
        vmem(NZ * TOK, WIDTH),
        vmem(NZ, 8, TOK, dtype=F32),
        vmem(2 * TOK, 2 * TOK),
        vmem(4, ROWS, 2 * TOK),
        vmem(4, ROWS, 128, dtype=F32),
        vmem(12 * PAIR, WIDTH),
        vmem(12 * PAIR, WIDTH),
        vmem(slots, WIDTH),
        vmem(slots, WIDTH),
        vmem(WIDTH, 2 * FF),
        vmem(FF, WIDTH),
        vmem(slots, FF),
        vmem(slots, 2 * FF),
        vmem(slots, WIDTH),
        vmem(slots, WIDTH),
        vmem(NZ * TOK, WIDTH, dtype=F32),
        vmem(2, 2, TOK, 256),
        vmem(7, 2, 2, TOK, 256),
        vmem(WIDTH, 2 * FF, dtype=F32),
        vmem(FF, WIDTH, dtype=F32),
        vmem(16, GU, 2 * FF),
        vmem(16, DN, WIDTH),
        [vmem(2, 4, 2, rows, WIDTH) for rows in PARTS],
        [vmem(rows, WIDTH) for rows in PARTS],
        [vmem(rows, WIDTH) for rows in PARTS],
        [vmem(rows, WIDTH) for rows in PARTS],
        [vmem(2, rows, WIDTH) for rows in PARTS],
        [vmem(NZ, rows, 128) for rows in PARTS],
        [vmem(NZ, rows, 128) for rows in PARTS],
        [vmem(NZ, rows, 128) for rows in PARTS],
        [vmem(NZ, rows, 128) for rows in PARTS],
        vmem(TOK, WIDTH),
        vmem(GU, 2 * FF, dtype=F32),
        vmem(DN, WIDTH, dtype=F32),
        pltpu.SemaphoreType.DMA((len(GROUPS),)),
        pltpu.SemaphoreType.DMA((RECEIVES,)),
        pltpu.SemaphoreType.DMA((8,)),
    ]
    in_vmem = pl.BlockSpec(memory_space=pltpu.VMEM)
    in_smem = pl.BlockSpec(memory_space=pltpu.SMEM)
    anywhere = pl.BlockSpec(memory_space=pl.ANY)
    results = pl.pallas_call(
        kernel,
        out_shape=(
            pltpu.VMEM((TOK, WIDTH), BF16),
            pltpu.VMEM((GU, 2 * FF), F32),
            pltpu.VMEM((DN, WIDTH), F32),
        ),
        in_specs=[in_vmem] * 2 + [anywhere] * 4 + [in_smem] * 2,
        out_specs=(anywhere,) * 3,
        scratch_shapes=scratch,
        compiler_params=pltpu.CompilerParams(
            collective_id=0, has_side_effects=True, vmem_limit_bytes=58 * 1024 * 1024
        ),
    )(expert_ids.T, gates.T, tokens, cotangent, w_gate_up, w_down, placement, partner)
    return pl.pallas_call(
        hand_on,
        out_shape=(
            jax.ShapeDtypeStruct((TOK, WIDTH), BF16),
            jax.ShapeDtypeStruct((1, GU, 2 * FF), F32),
            jax.ShapeDtypeStruct((1, DN, WIDTH), F32),
        ),
        in_specs=[in_vmem] * 3,
        out_specs=(anywhere,) * 3,
        scratch_shapes=[pltpu.SemaphoreType.DMA((3,))],
        compiler_params=pltpu.CompilerParams(vmem_limit_bytes=1024 * 1024),
    )(*results)


def solution(mesh):
    return jax.shard_map(
        body,
        mesh=mesh,
        in_specs=(
            P(("dp", "expert"), None),
            P(("dp", "expert"), None),
            P(("dp", "expert"), None),
            P(("dp", "expert"), None),
            P(),
            P(),
            P("expert", "dp", None),
            P("expert", "dp", None),
        ),
        out_specs=(P(("dp", "expert"), None), P("expert", "dp", None), P("expert", "dp", None)),
        check_vma=False,
    )
```

time: 125 us -> 116 us (0.928)
  the two profiles are of different devices: /device:TPU:152 before, /device:TPU:2 now
where the time goes in v3:
time: 116 us
  Pallas kernels  116 us (100%)
    pallas_call x1, Pallas kernels, body(): pl.pallas_call(kernel, out_shape=(pltpu.VMEM((TOK, WIDTH), BF16), pltpu.V...  115 us

profile of v3, /device:TPU:2, one launch (start us, length us, event | category | flops | bytes accessed | tf_op | source)
XLA Modules:
  0.0 116.2 jit_solution(14497149747538271173)
XLA Ops:
  0.6 114.8 %shard_map.103 = (bf16[128,1024]{1,0:T(8,128)(2,1)S(1)}, f32[64,1024]{1,0:T(8,128)S(1)}, f32[32,1024]{1,0:T(8,128)S(1)}) custom-call(s32[4,128]{1,0:T(4,128)} %bitcast.2, f32[4,128]{1,0:T(4,128)} %bitcast.3, bf16[128,1024]{1,0:T(8,128)(2,1)} %tok_ref.1, bf16[128,1024]{1,0:T(8,128)(2,1)} %cot_ref.1, bf16[1,64,1024]{2,1,0:T(8,128)(2,1)} %gu_ref.1, ...), custom_call_target="tpu_custom_call" | custom-call | tf_op jit(solution)/shard_map/pallas_call | solution.py:619
  115.4 0.9 shard_map.104

commit v4 on v3

--- a/solution.py
+++ b/solution.py
@@ -48,7 +48,7 @@
     ids_ref, gates_ref, tok_ref, cot_ref, gu_ref, dn_ref, placement_ref, partner_ref,
     tg_out, gu_out, dn_out,
     gx, gc, gm, tri, sel, gcol, stx, stu, ex, eu, wgu, wdn, hb, qb, bk, rb,
-    tgp, sz, rz, agu, adn, pgu, pdn, ry, tx, rx, sl, rl, cut, via, onward, whence, tgb, gub, dnb,
+    tgp, sz, rz, agu, adn, pgu, pdn, ry, tx, rx, sl, rl, cut, via, onward, whence,
     ssem, rsem, lsem,
 ):
     dpi = lax.axis_index("dp")
@@ -258,6 +258,9 @@
             hb[rows, cols] = (active * b).astype(BF16)
             qb[rows, cols] = (dh * b * (s * (1.0 + a * (1.0 - s)))).astype(BF16)
             qb[rows, up_cols] = (dh * active).astype(BF16)
+
+    def expert_back(pair):
+        rows = slice(pair * ROWS, (pair + 1) * ROWS)
         for tile in range(0, WIDTH, 256):
             cols = pl.ds(tile, 256)
             value = dot(qb[rows], wgu[cols], LAST_LAST).astype(BF16)
@@ -302,8 +305,7 @@
             for index, _, _ in ways:
                 low = index * 512 + half * 256
                 total = tgp[OWN * TOK :, low : low + 256] + rz[6, half, index].astype(F32)
-                tgb[:, low : low + 256] = total.astype(BF16)
-        move(tgb, tg_out)
+                tg_out[:, low : low + 256] = total.astype(BF16)
 
     parts = {"dn": (pdn, 0, PARTS[0]), "g0": (pgu, 0, PARTS[1]), "g1": (pgu, 32, PARTS[2])}
     kinds = list(parts)
@@ -345,7 +347,7 @@
             total = total + landed.astype(F32)
         return total
 
-    results = {"dn": (dnb, dn_out, 0), "g0": (gub, gu_out, 0), "g1": (gub, gu_out, 32)}
+    results = {"dn": (dn_out, 0), "g0": (gu_out, 0), "g1": (gu_out, 32)}
     crossed, moved, spread, reached = {}, {}, {}, {}
 
     def grad_cross(kind):
@@ -356,7 +358,7 @@
 
     def grad_swap(kind):
         index = kinds.index(kind)
-        kept, _, start = results[kind]
+        kept, start = results[kind]
         total = grad_sum(kind, "own")
         arrive(crossed[kind], rx[index])
         total = total + rx[index][...].astype(F32)
@@ -392,7 +394,7 @@
 
     def grad_last(kind):
         index = kinds.index(kind)
-        kept, out, start = results[kind]
+        kept, start = results[kind]
         mate = partner_ref[ei]
         arrive(moved[kind], rl[index])
         arrive(reached[kind], whence[index].at[pl.ds(1, NZ - 1)])
@@ -402,8 +404,6 @@
         pieces = [whence[index][piece].astype(F32) for piece in range(NZ)]
         value = jnp.where(lax.div(mate, 4) == z, value, jnp.concatenate(pieces, axis=1))
         kept[start : start + PARTS[index], :] = value
-        place = pl.ds(start, PARTS[index])
-        move(kept.at[place], out.at[place])
 
     early = 3 * ROWS
 
@@ -463,14 +463,17 @@
     last_weights("oth")
     rows_here(0)
     expert(0)
+    expert_back(0)
     block_here("x", 4)
     dispatch("x", 3)
     rows_here(1)
     expert(1)
+    expert_back(1)
     block_here("c", 4)
     dispatch("c", 3)
     rows_here(2)
     expert(2)
+    expert_back(2)
     ahead_of_last()
     rows_here(3)
     give_back(0)
@@ -495,6 +498,7 @@
     grad_round("dn", "own", 3)
     token_step(2, 0)
     grad_round("g0", "own", 1)
+    expert_back(3)
     give_back(3)
     combine(2)
     grad_round("dn", "oth", 3)
@@ -535,8 +539,6 @@
     grad_last("dn")
     grad_last("g1")
     grad_last("g0")
-    for copy in local[len(own_parts) :]:
-        copy.wait()
     for group, sources in sent.items():
         size = sum(math.prod(source.shape) for source in sources)
         if group == "meta":
@@ -606,12 +608,9 @@
         [vmem(NZ, rows, 128) for rows in PARTS],
         [vmem(NZ, rows, 128) for rows in PARTS],
         [vmem(NZ, rows, 128) for rows in PARTS],
-        vmem(TOK, WIDTH),
-        vmem(GU, 2 * FF, dtype=F32),
-        vmem(DN, WIDTH, dtype=F32),
         pltpu.SemaphoreType.DMA((len(GROUPS),)),
         pltpu.SemaphoreType.DMA((RECEIVES,)),
-        pltpu.SemaphoreType.DMA((8,)),
+        pltpu.SemaphoreType.DMA((4,)),
     ]
     in_vmem = pl.BlockSpec(memory_space=pltpu.VMEM)
     in_smem = pl.BlockSpec(memory_space=pltpu.SMEM)
@@ -624,7 +623,7 @@
             pltpu.VMEM((DN, WIDTH), F32),
         ),
         in_specs=[in_vmem] * 2 + [anywhere] * 4 + [in_smem] * 2,
-        out_specs=(anywhere,) * 3,
+        out_specs=(in_vmem,) * 3,
         scratch_shapes=scratch,
         compiler_params=pltpu.CompilerParams(
             collective_id=0, has_side_effects=True, vmem_limit_bytes=58 * 1024 * 1024

time: 116 us -> 116 us (level)
  the two profiles are of different devices: /device:TPU:2 before, /device:TPU:20 now
where the time goes in v4:
time: 116 us
  Pallas kernels  115 us (99%)
    pallas_call x1, Pallas kernels, body(): pl.pallas_call(kernel, out_shape=(pltpu.VMEM((TOK, WIDTH), BF16), pltpu.V...  114 us

profile of v4, /device:TPU:20, one launch (start us, length us, event | category | flops | bytes accessed | tf_op | source)
XLA Modules:
  0.0 115.7 jit_solution(1520519390944930432)
XLA Ops:
  0.6 114.2 %shard_map.103 = (bf16[128,1024]{1,0:T(8,128)(2,1)S(1)}, f32[64,1024]{1,0:T(8,128)S(1)}, f32[32,1024]{1,0:T(8,128)S(1)}) custom-call(s32[4,128]{1,0:T(4,128)} %bitcast.2, f32[4,128]{1,0:T(4,128)} %bitcast.3, bf16[128,1024]{1,0:T(8,128)(2,1)} %tok_ref.1, bf16[128,1024]{1,0:T(8,128)(2,1)} %cot_ref.1, bf16[1,64,1024]{2,1,0:T(8,128)(2,1)} %gu_ref.1, ...), custom_call_target="tpu_custom_call" | custom-call | tf_op jit(solution)/shard_map/pallas_call | solution.py:618
  114.8 0.9 shard_map.104

commit v5 on v4

--- a/solution.py
+++ b/solution.py
@@ -135,11 +135,6 @@
         for way in (1, -1):
             arrive(coming[side, way, reach[side, way]], one_slice)
 
-    across = new()
-    for buffer, rows, mine in whole.values():
-        send("weights", across, mine, slice_at(buffer, rows, xl, 0), other_side)
-    pass_weights("own", 1)
-
     def block(ref, index):
         return ref.at[pl.ds(index * TOK, TOK)]
 
@@ -173,6 +168,8 @@
                 source, target = source.at[part], target.at[part]
             send("ring", ring[name, hop], source, target, zdev(way))
 
+    pass_block("x", 1)
+
     ids = ids_ref[...]
     holder = jnp.zeros(ids.shape, F32)
     for e in range(32):
@@ -180,8 +177,11 @@
     gm[OWN, 0:4, :] = holder
     gm[OWN, 4:8, :] = gates_ref[...]
     pass_meta(1)
-    pass_block("x", 1)
     pass_block("c", 1)
+    across = new()
+    for buffer, rows, mine in whole.values():
+        send("weights", across, mine, slice_at(buffer, rows, xl, 0), other_side)
+    pass_weights("own", 1)
     own_parts = [move(tok_ref, block(gx, OWN)), move(cot_ref, block(gc, OWN))]
     for buffer, rows, mine in whole.values():
         own_parts.append(move(mine, slice_at(buffer, rows, xl, 0)))

time: 116 us -> 116 us (level)
  the two profiles are of different devices: /device:TPU:20 before, /device:TPU:14 now
where the time goes in v5:
time: 116 us
  Pallas kernels  115 us (99%)
    pallas_call x1, Pallas kernels, body(): pl.pallas_call(kernel, out_shape=(pltpu.VMEM((TOK, WIDTH), BF16), pltpu.V...  114 us

profile of v5, /device:TPU:14, one launch (start us, length us, event | category | flops | bytes accessed | tf_op | source)
XLA Modules:
  0.0 115.6 jit_solution(852817783814093965)
XLA Ops:
  0.6 114.2 %shard_map.103 = (bf16[128,1024]{1,0:T(8,128)(2,1)S(1)}, f32[64,1024]{1,0:T(8,128)S(1)}, f32[32,1024]{1,0:T(8,128)S(1)}) custom-call(s32[4,128]{1,0:T(4,128)} %bitcast.2, f32[4,128]{1,0:T(4,128)} %bitcast.3, bf16[128,1024]{1,0:T(8,128)(2,1)} %tok_ref.1, bf16[128,1024]{1,0:T(8,128)(2,1)} %cot_ref.1, bf16[1,64,1024]{2,1,0:T(8,128)(2,1)} %gu_ref.1, ...), custom_call_target="tpu_custom_call" | custom-call | tf_op jit(solution)/shard_map/pallas_call | solution.py:618
  114.8 0.9 shard_map.104
